TPU v7x, 256 devices: a whole 4x4x8 slice. The times are simulated.
256 devices in a mesh: ctx: 32 (over z, x_lo, core), section: 8 (over y, x_hi).
Axes of the slice: x: 4 (x_hi: 2, x_lo: 2; x = x_hi * 2 + x_lo), y: 4, z: 8, core: 2. Of those that a mesh axis runs over, the one named last changes fastest.
Arguments:
- queries: bfloat16 [8, 8192, 4608], P('section', 'ctx'), may hold values from -32 to 32
- latent_cache: bfloat16 [8, 576, 8192], P('section', None, 'ctx'), may hold values from -4 to 4
- doc_ids: int32 [8, 8192], P('section', 'ctx'), may hold values from 0 to 7, never falling along the last dimension, each value on 1 to 6144 neighbouring positions
- block_table: int32 [32, 32], replicated, may hold values 0 or 1
- w_uv: bfloat16 [8, 8, 512, 128], P('section'), may hold values from -0.5 to 0.5
Outputs:
- handed: bfloat16 [8, 8192, 1024], P('section', 'ctx')
Inputs may be any that keep to these rules, and one draw needn't show every extreme that they name: `doc_ids`: along each layer's 8192 tokens the document ids never fall.
All inputs are finite; a program needn't handle non-finite values.
Results may differ from a plain program's by a relative error of at most 0.009.
Values may be sent and summed in bfloat16 or wider, within the bound.
No kernel may reach another device: no remote copies, remote signals or barrier semaphores. Data moves between devices by JAX's collectives and lax.ppermute only.
A program may use at most 64 MiB of HBM per device.

v0:
```python
import jax
import jax.numpy as jnp
from jax import lax
from jax.sharding import PartitionSpec as P

very_low = -1e30


def from_behind(x, axis, by):
    peers = lax.axis_size(axis)
    return lax.ppermute(x, axis, [(i, (i + by) % peers) for i in range(peers)])


def attend_block(
    carried,
    query_rows,
    query_ids,
    query_block,
    table_row,
    cache_block,
    key_ids,
    key_start,
    latent_width,
    score_scale,
):
    tokens_q = query_ids.shape[0]
    heads_q = query_rows.shape[0] // tokens_q
    key_count = cache_block.shape[1]
    key_block = key_start // tokens_q
    table_hit = jnp.sum(
        jnp.where(jnp.arange(table_row.shape[0], dtype=jnp.int32) == key_block, table_row, 0)
    )
    opened = (table_hit == 1) | (key_block == query_block)
    is_live = (key_block == query_block) | (key_block < query_block) & (table_hit == 1) & (
        key_ids[-1] >= query_ids[0]
    )

    def compute(current):
        peak_old, total_old, accum_old = current
        scores = jnp.dot(query_rows, cache_block, preferred_element_type=jnp.float32) * score_scale
        scores = scores.reshape(tokens_q, heads_q, key_count)
        query_pos = query_block * tokens_q + jnp.arange(tokens_q, dtype=jnp.int32)
        key_pos = key_start + jnp.arange(key_count, dtype=jnp.int32)
        allowed = (
            (query_ids[:, None] == key_ids[None, :])
            & (key_pos[None, :] <= query_pos[:, None])
            & opened
        )
        allowed = allowed[:, None, :]
        scores = jnp.where(allowed, scores, very_low)
        peak_new = jnp.maximum(peak_old, jnp.max(scores, axis=2))
        weights = jnp.where(allowed, jnp.exp(scores - peak_new[:, :, None]), 0.0)
        factor = jnp.exp(peak_old - peak_new)
        total_new = total_old * factor + jnp.sum(weights, axis=2)
        weights_low = weights.astype(jnp.bfloat16).reshape(tokens_q * heads_q, key_count)
        values = cache_block[:latent_width]
        mixed_part = lax.dot_general(
            weights_low, values, (((1,), (1,)), ((), ())), preferred_element_type=jnp.float32
        )
        accum_new = accum_old * factor.reshape(-1, 1) + mixed_part
        return (peak_new, total_new, accum_new)

    return lax.cond(is_live, compute, lambda current: current, carried)


def finish(final_state, weights_uv):
    row_peak, row_total, row_accum = final_state
    tokens_q, heads_q = row_total.shape
    mixed_rows = (
        (row_accum / row_total.reshape(-1, 1)).astype(jnp.bfloat16).reshape(tokens_q, heads_q, -1)
    )
    projected = jnp.einsum(
        "thl,hlv->thv", mixed_rows, weights_uv, preferred_element_type=jnp.float32
    )
    return projected.reshape(tokens_q, -1).astype(jnp.bfloat16)


def shards(queries, latent_cache, doc_ids, block_table, w_uv):
    tokens_here = queries.shape[1]
    heads_count = w_uv.shape[1]
    latent_width = w_uv.shape[2]
    value_width = w_uv.shape[3]
    cache_width = latent_cache.shape[1]
    rope_width = cache_width - latent_width
    score_scale = (value_width + rope_width) ** (-0.5)
    cycle_count = lax.axis_size("ctx")
    query_block = lax.axis_index("ctx")
    query_rows = queries[0].reshape(tokens_here * heads_count, cache_width)
    query_ids = doc_ids[0]
    block_numbers = jnp.arange(cycle_count, dtype=jnp.int32)
    table_row = jnp.sum(jnp.where(block_numbers[:, None] == query_block, block_table, 0), axis=0)
    initial = (
        jnp.full((tokens_here, heads_count), very_low, jnp.float32),
        jnp.zeros((tokens_here, heads_count), jnp.float32),
        jnp.zeros((tokens_here * heads_count, latent_width), jnp.float32),
    )

    def visit(carried, cache_block, key_ids, key_start):
        return attend_block(
            carried,
            query_rows,
            query_ids,
            query_block,
            table_row,
            cache_block,
            key_ids,
            key_start,
            latent_width,
            score_scale,
        )

    cache_piece = lax.all_gather(latent_cache, "ctx", axis=2, tiled=True)[0]
    id_piece = lax.all_gather(doc_ids[:, None, :], "ctx", axis=2, tiled=True)[0, 0]
    width_piece = cache_piece.shape[1]
    step_size = min(width_piece, tokens_here)

    def over_steps(position, carried):
        first_row = position * step_size
        cache_step = lax.dynamic_slice_in_dim(cache_piece, first_row, step_size, 1)
        id_step = lax.dynamic_slice_in_dim(id_piece, first_row, step_size, 0)
        return visit(carried, cache_step, id_step, first_row)

    final_state = lax.fori_loop(0, width_piece // step_size, over_steps, initial)
    heads_out = finish(final_state, w_uv[0])
    return from_behind(heads_out[None], "section", 1)


def solution(mesh):
    placed = (
        P("section", "ctx", None),
        P("section", None, "ctx"),
        P("section", "ctx"),
        P(),
        P("section", None, None, None),
    )
    return jax.shard_map(
        shards, mesh=mesh, in_specs=placed, out_specs=P("section", "ctx", None), check_vma=False
    )
```

profile of v0, /device:TPU:224, one launch (start us, length us, event | category | flops | bytes accessed | tf_op | source)
XLA Modules:
  0.0 624.9 jit_solution(825981962687086034)
XLA Ops:
  7.3 5.5 reshape_squeeze.3
  12.8 32.8 %all-gather = s32[1,8192]{1,0:T(1,128)} all-gather(s32[1,256]{1,0:T(1,128)S(1)} %copy-done.2), channel_id=2, replica_groups=mesh['ctx'=32,'section'=8] {'ctx'}, dimensions={1}, use_global_device_ids=true | all-gather | bytes 33792 | tf_op jit(solution)/shard_map/all_gather | solution.py:113
  46.3 56.5 %all-gather.3.cloned.1.call-done = bf16[1,576,8192]{2,1,0:T(8,128)(2,1)} async-done(((bf16[1,576,256]{2,1,0:T(8,128)(2,1)}), bf16[1,576,8192]{2,1,0:T(8,128)(2,1)}) %all-gather.3.cloned.1.call-update) | async-done | bytes 9437200 | tf_op jit(solution)/shard_map/all_gather | solution.py:112
  106.1 493.6 %while.19 = (s32[]{:T(128)}, f32[256,8]{1,0:T(8,128)S(1)}, f32[256,8]{1,0:T(8,128)}, f32[2048,512]{1,0:T(8,128)}, s32[]{:T(128)}, /*index=5*/s32[32]{0:T(128)}, ...) while((s32[]{:T(128)}, f32[256,8]{1,0:T(8,128)S(1)}, ...), condition=%wide.region_7.8_spmd, body=%wide.region_1.7_spmd.sunk | while | flops 1147933312 | bytes 23439096 | solution.py:123
  132.1 14.3 %conditional.2 = ((f32[256,8]{1,0:T(8,128)S(1)}, f32[256,8]{1,0:T(8,128)}, f32[2048,512]{1,0:T(8,128)})) conditional(s32[]{:T(128)} %convert_element_type.45, (f32[256,8]{1,0:T(8,128)S(1)}, f32[256,8]{1,0:T(8,128)}, f32[2048,512]{1,0:T(8,128)}) %tuple.50, (s32[1,256]{1,0:T(1,128)S(1)}, s32[256]{0:T(256)S(1)}, s32[]{:T(128)}, s32[]{:T(128)}, ...), branch_computations={%region_3.3_spmd, %region_4.6_spmd} | conditional | flops 1147933184 | bytes 23436372 | solution.py:63
  133.2 3.2 fusion.20
  140.7 5.7 multiply_add_fusion
  151.6 14.3 %conditional.2 = ((f32[256,8]{1,0:T(8,128)S(1)}, f32[256,8]{1,0:T(8,128)}, f32[2048,512]{1,0:T(8,128)})) conditional(s32[]{:T(128)} %convert_element_type.45, (f32[256,8]{1,0:T(8,128)S(1)}, f32[256,8]{1,0:T(8,128)}, f32[2048,512]{1,0:T(8,128)}) %tuple.50, (s32[1,256]{1,0:T(1,128)S(1)}, s32[256]{0:T(256)S(1)}, s32[]{:T(128)}, s32[]{:T(128)}, ...), branch_computations={%region_3.3_spmd, %region_4.6_spmd} | conditional | flops 1147933184 | bytes 23436372 | solution.py:63
  152.6 3.2 fusion.20
  160.1 5.7 multiply_add_fusion
  171.0 14.3 %conditional.2 = ((f32[256,8]{1,0:T(8,128)S(1)}, f32[256,8]{1,0:T(8,128)}, f32[2048,512]{1,0:T(8,128)})) conditional(s32[]{:T(128)} %convert_element_type.45, (f32[256,8]{1,0:T(8,128)S(1)}, f32[256,8]{1,0:T(8,128)}, f32[2048,512]{1,0:T(8,128)}) %tuple.50, (s32[1,256]{1,0:T(1,128)S(1)}, s32[256]{0:T(256)S(1)}, s32[]{:T(128)}, s32[]{:T(128)}, ...), branch_computations={%region_3.3_spmd, %region_4.6_spmd} | conditional | flops 1147933184 | bytes 23436372 | solution.py:63
  179.6 5.7 multiply_add_fusion
  190.4 14.3 %conditional.2 = ((f32[256,8]{1,0:T(8,128)S(1)}, f32[256,8]{1,0:T(8,128)}, f32[2048,512]{1,0:T(8,128)})) conditional(s32[]{:T(128)} %convert_element_type.45, (f32[256,8]{1,0:T(8,128)S(1)}, f32[256,8]{1,0:T(8,128)}, f32[2048,512]{1,0:T(8,128)}) %tuple.50, (s32[1,256]{1,0:T(1,128)S(1)}, s32[256]{0:T(256)S(1)}, s32[]{:T(128)}, s32[]{:T(128)}, ...), branch_computations={%region_3.3_spmd, %region_4.6_spmd} | conditional | flops 1147933184 | bytes 23436372 | solution.py:63
  199.0 5.7 multiply_add_fusion
  215.1 14.3 %conditional.2 = ((f32[256,8]{1,0:T(8,128)S(1)}, f32[256,8]{1,0:T(8,128)}, f32[2048,512]{1,0:T(8,128)})) conditional(s32[]{:T(128)} %convert_element_type.45, (f32[256,8]{1,0:T(8,128)S(1)}, f32[256,8]{1,0:T(8,128)}, f32[2048,512]{1,0:T(8,128)}) %tuple.50, (s32[1,256]{1,0:T(1,128)S(1)}, s32[256]{0:T(256)S(1)}, s32[]{:T(128)}, s32[]{:T(128)}, ...), branch_computations={%region_3.3_spmd, %region_4.6_spmd} | conditional | flops 1147933184 | bytes 23436372 | solution.py:63
  216.1 3.2 fusion.20
  223.6 5.7 multiply_add_fusion
  234.5 14.3 %conditional.2 = ((f32[256,8]{1,0:T(8,128)S(1)}, f32[256,8]{1,0:T(8,128)}, f32[2048,512]{1,0:T(8,128)})) conditional(s32[]{:T(128)} %convert_element_type.45, (f32[256,8]{1,0:T(8,128)S(1)}, f32[256,8]{1,0:T(8,128)}, f32[2048,512]{1,0:T(8,128)}) %tuple.50, (s32[1,256]{1,0:T(1,128)S(1)}, s32[256]{0:T(256)S(1)}, s32[]{:T(128)}, s32[]{:T(128)}, ...), branch_computations={%region_3.3_spmd, %region_4.6_spmd} | conditional | flops 1147933184 | bytes 23436372 | solution.py:63
  235.6 3.2 fusion.20
  243.0 5.7 multiply_add_fusion
  253.9 14.3 %conditional.2 = ((f32[256,8]{1,0:T(8,128)S(1)}, f32[256,8]{1,0:T(8,128)}, f32[2048,512]{1,0:T(8,128)})) conditional(s32[]{:T(128)} %convert_element_type.45, (f32[256,8]{1,0:T(8,128)S(1)}, f32[256,8]{1,0:T(8,128)}, f32[2048,512]{1,0:T(8,128)}) %tuple.50, (s32[1,256]{1,0:T(1,128)S(1)}, s32[256]{0:T(256)S(1)}, s32[]{:T(128)}, s32[]{:T(128)}, ...), branch_computations={%region_3.3_spmd, %region_4.6_spmd} | conditional | flops 1147933184 | bytes 23436372 | solution.py:63
  255.0 3.2 fusion.20
  262.5 5.7 multiply_add_fusion
  273.3 14.3 %conditional.2 = ((f32[256,8]{1,0:T(8,128)S(1)}, f32[256,8]{1,0:T(8,128)}, f32[2048,512]{1,0:T(8,128)})) conditional(s32[]{:T(128)} %convert_element_type.45, (f32[256,8]{1,0:T(8,128)S(1)}, f32[256,8]{1,0:T(8,128)}, f32[2048,512]{1,0:T(8,128)}) %tuple.50, (s32[1,256]{1,0:T(1,128)S(1)}, s32[256]{0:T(256)S(1)}, s32[]{:T(128)}, s32[]{:T(128)}, ...), branch_computations={%region_3.3_spmd, %region_4.6_spmd} | conditional | flops 1147933184 | bytes 23436372 | solution.py:63
  281.9 5.7 multiply_add_fusion
  292.7 14.3 %conditional.2 = ((f32[256,8]{1,0:T(8,128)S(1)}, f32[256,8]{1,0:T(8,128)}, f32[2048,512]{1,0:T(8,128)})) conditional(s32[]{:T(128)} %convert_element_type.45, (f32[256,8]{1,0:T(8,128)S(1)}, f32[256,8]{1,0:T(8,128)}, f32[2048,512]{1,0:T(8,128)}) %tuple.50, (s32[1,256]{1,0:T(1,128)S(1)}, s32[256]{0:T(256)S(1)}, s32[]{:T(128)}, s32[]{:T(128)}, ...), branch_computations={%region_3.3_spmd, %region_4.6_spmd} | conditional | flops 1147933184 | bytes 23436372 | solution.py:63
  293.8 3.2 fusion.20
  301.3 5.7 multiply_add_fusion
  312.1 14.3 %conditional.2 = ((f32[256,8]{1,0:T(8,128)S(1)}, f32[256,8]{1,0:T(8,128)}, f32[2048,512]{1,0:T(8,128)})) conditional(s32[]{:T(128)} %convert_element_type.45, (f32[256,8]{1,0:T(8,128)S(1)}, f32[256,8]{1,0:T(8,128)}, f32[2048,512]{1,0:T(8,128)}) %tuple.50, (s32[1,256]{1,0:T(1,128)S(1)}, s32[256]{0:T(256)S(1)}, s32[]{:T(128)}, s32[]{:T(128)}, ...), branch_computations={%region_3.3_spmd, %region_4.6_spmd} | conditional | flops 1147933184 | bytes 23436372 | solution.py:63
  320.7 5.7 multiply_add_fusion
  331.6 14.3 %conditional.2 = ((f32[256,8]{1,0:T(8,128)S(1)}, f32[256,8]{1,0:T(8,128)}, f32[2048,512]{1,0:T(8,128)})) conditional(s32[]{:T(128)} %convert_element_type.45, (f32[256,8]{1,0:T(8,128)S(1)}, f32[256,8]{1,0:T(8,128)}, f32[2048,512]{1,0:T(8,128)}) %tuple.50, (s32[1,256]{1,0:T(1,128)S(1)}, s32[256]{0:T(256)S(1)}, s32[]{:T(128)}, s32[]{:T(128)}, ...), branch_computations={%region_3.3_spmd, %region_4.6_spmd} | conditional | flops 1147933184 | bytes 23436372 | solution.py:63
  332.6 3.2 fusion.20
  340.1 5.7 multiply_add_fusion
  351.0 14.3 %conditional.2 = ((f32[256,8]{1,0:T(8,128)S(1)}, f32[256,8]{1,0:T(8,128)}, f32[2048,512]{1,0:T(8,128)})) conditional(s32[]{:T(128)} %convert_element_type.45, (f32[256,8]{1,0:T(8,128)S(1)}, f32[256,8]{1,0:T(8,128)}, f32[2048,512]{1,0:T(8,128)}) %tuple.50, (s32[1,256]{1,0:T(1,128)S(1)}, s32[256]{0:T(256)S(1)}, s32[]{:T(128)}, s32[]{:T(128)}, ...), branch_computations={%region_3.3_spmd, %region_4.6_spmd} | conditional | flops 1147933184 | bytes 23436372 | solution.py:63
  359.5 5.7 multiply_add_fusion
  370.4 14.3 %conditional.2 = ((f32[256,8]{1,0:T(8,128)S(1)}, f32[256,8]{1,0:T(8,128)}, f32[2048,512]{1,0:T(8,128)})) conditional(s32[]{:T(128)} %convert_element_type.45, (f32[256,8]{1,0:T(8,128)S(1)}, f32[256,8]{1,0:T(8,128)}, f32[2048,512]{1,0:T(8,128)}) %tuple.50, (s32[1,256]{1,0:T(1,128)S(1)}, s32[256]{0:T(256)S(1)}, s32[]{:T(128)}, s32[]{:T(128)}, ...), branch_computations={%region_3.3_spmd, %region_4.6_spmd} | conditional | flops 1147933184 | bytes 23436372 | solution.py:63
  371.4 3.2 fusion.20
  378.9 5.7 multiply_add_fusion
  395.0 14.3 %conditional.2 = ((f32[256,8]{1,0:T(8,128)S(1)}, f32[256,8]{1,0:T(8,128)}, f32[2048,512]{1,0:T(8,128)})) conditional(s32[]{:T(128)} %convert_element_type.45, (f32[256,8]{1,0:T(8,128)S(1)}, f32[256,8]{1,0:T(8,128)}, f32[2048,512]{1,0:T(8,128)}) %tuple.50, (s32[1,256]{1,0:T(1,128)S(1)}, s32[256]{0:T(256)S(1)}, s32[]{:T(128)}, s32[]{:T(128)}, ...), branch_computations={%region_3.3_spmd, %region_4.6_spmd} | conditional | flops 1147933184 | bytes 23436372 | solution.py:63
  403.5 5.7 multiply_add_fusion
  414.4 14.3 %conditional.2 = ((f32[256,8]{1,0:T(8,128)S(1)}, f32[256,8]{1,0:T(8,128)}, f32[2048,512]{1,0:T(8,128)})) conditional(s32[]{:T(128)} %convert_element_type.45, (f32[256,8]{1,0:T(8,128)S(1)}, f32[256,8]{1,0:T(8,128)}, f32[2048,512]{1,0:T(8,128)}) %tuple.50, (s32[1,256]{1,0:T(1,128)S(1)}, s32[256]{0:T(256)S(1)}, s32[]{:T(128)}, s32[]{:T(128)}, ...), branch_computations={%region_3.3_spmd, %region_4.6_spmd} | conditional | flops 1147933184 | bytes 23436372 | solution.py:63
  415.5 3.2 fusion.20
  423.0 5.7 multiply_add_fusion
  433.8 14.3 %conditional.2 = ((f32[256,8]{1,0:T(8,128)S(1)}, f32[256,8]{1,0:T(8,128)}, f32[2048,512]{1,0:T(8,128)})) conditional(s32[]{:T(128)} %convert_element_type.45, (f32[256,8]{1,0:T(8,128)S(1)}, f32[256,8]{1,0:T(8,128)}, f32[2048,512]{1,0:T(8,128)}) %tuple.50, (s32[1,256]{1,0:T(1,128)S(1)}, s32[256]{0:T(256)S(1)}, s32[]{:T(128)}, s32[]{:T(128)}, ...), branch_computations={%region_3.3_spmd, %region_4.6_spmd} | conditional | flops 1147933184 | bytes 23436372 | solution.py:63
  434.9 3.2 fusion.20
  442.4 5.7 multiply_add_fusion
  453.3 14.3 %conditional.2 = ((f32[256,8]{1,0:T(8,128)S(1)}, f32[256,8]{1,0:T(8,128)}, f32[2048,512]{1,0:T(8,128)})) conditional(s32[]{:T(128)} %convert_element_type.45, (f32[256,8]{1,0:T(8,128)S(1)}, f32[256,8]{1,0:T(8,128)}, f32[2048,512]{1,0:T(8,128)}) %tuple.50, (s32[1,256]{1,0:T(1,128)S(1)}, s32[256]{0:T(256)S(1)}, s32[]{:T(128)}, s32[]{:T(128)}, ...), branch_computations={%region_3.3_spmd, %region_4.6_spmd} | conditional | flops 1147933184 | bytes 23436372 | solution.py:63
  454.3 3.2 fusion.20
  461.8 5.7 multiply_add_fusion
  472.7 14.3 %conditional.2 = ((f32[256,8]{1,0:T(8,128)S(1)}, f32[256,8]{1,0:T(8,128)}, f32[2048,512]{1,0:T(8,128)})) conditional(s32[]{:T(128)} %convert_element_type.45, (f32[256,8]{1,0:T(8,128)S(1)}, f32[256,8]{1,0:T(8,128)}, f32[2048,512]{1,0:T(8,128)}) %tuple.50, (s32[1,256]{1,0:T(1,128)S(1)}, s32[256]{0:T(256)S(1)}, s32[]{:T(128)}, s32[]{:T(128)}, ...), branch_computations={%region_3.3_spmd, %region_4.6_spmd} | conditional | flops 1147933184 | bytes 23436372 | solution.py:63
  473.8 3.2 fusion.20
  481.3 5.7 multiply_add_fusion
  492.1 14.3 %conditional.2 = ((f32[256,8]{1,0:T(8,128)S(1)}, f32[256,8]{1,0:T(8,128)}, f32[2048,512]{1,0:T(8,128)})) conditional(s32[]{:T(128)} %convert_element_type.45, (f32[256,8]{1,0:T(8,128)S(1)}, f32[256,8]{1,0:T(8,128)}, f32[2048,512]{1,0:T(8,128)}) %tuple.50, (s32[1,256]{1,0:T(1,128)S(1)}, s32[256]{0:T(256)S(1)}, s32[]{:T(128)}, s32[]{:T(128)}, ...), branch_computations={%region_3.3_spmd, %region_4.6_spmd} | conditional | flops 1147933184 | bytes 23436372 | solution.py:63
  493.2 3.2 fusion.20
  500.7 5.7 multiply_add_fusion
  511.5 14.3 %conditional.2 = ((f32[256,8]{1,0:T(8,128)S(1)}, f32[256,8]{1,0:T(8,128)}, f32[2048,512]{1,0:T(8,128)})) conditional(s32[]{:T(128)} %convert_element_type.45, (f32[256,8]{1,0:T(8,128)S(1)}, f32[256,8]{1,0:T(8,128)}, f32[2048,512]{1,0:T(8,128)}) %tuple.50, (s32[1,256]{1,0:T(1,128)S(1)}, s32[256]{0:T(256)S(1)}, s32[]{:T(128)}, s32[]{:T(128)}, ...), branch_computations={%region_3.3_spmd, %region_4.6_spmd} | conditional | flops 1147933184 | bytes 23436372 | solution.py:63
  520.1 5.7 multiply_add_fusion
  531.0 14.3 %conditional.2 = ((f32[256,8]{1,0:T(8,128)S(1)}, f32[256,8]{1,0:T(8,128)}, f32[2048,512]{1,0:T(8,128)})) conditional(s32[]{:T(128)} %convert_element_type.45, (f32[256,8]{1,0:T(8,128)S(1)}, f32[256,8]{1,0:T(8,128)}, f32[2048,512]{1,0:T(8,128)}) %tuple.50, (s32[1,256]{1,0:T(1,128)S(1)}, s32[256]{0:T(256)S(1)}, s32[]{:T(128)}, s32[]{:T(128)}, ...), branch_computations={%region_3.3_spmd, %region_4.6_spmd} | conditional | flops 1147933184 | bytes 23436372 | solution.py:63
  539.5 5.7 multiply_add_fusion
  550.4 14.3 %conditional.2 = ((f32[256,8]{1,0:T(8,128)S(1)}, f32[256,8]{1,0:T(8,128)}, f32[2048,512]{1,0:T(8,128)})) conditional(s32[]{:T(128)} %convert_element_type.45, (f32[256,8]{1,0:T(8,128)S(1)}, f32[256,8]{1,0:T(8,128)}, f32[2048,512]{1,0:T(8,128)}) %tuple.50, (s32[1,256]{1,0:T(1,128)S(1)}, s32[256]{0:T(256)S(1)}, s32[]{:T(128)}, s32[]{:T(128)}, ...), branch_computations={%region_3.3_spmd, %region_4.6_spmd} | conditional | flops 1147933184 | bytes 23436372 | solution.py:63
  558.9 5.7 multiply_add_fusion
  569.8 14.3 %conditional.2 = ((f32[256,8]{1,0:T(8,128)S(1)}, f32[256,8]{1,0:T(8,128)}, f32[2048,512]{1,0:T(8,128)})) conditional(s32[]{:T(128)} %convert_element_type.45, (f32[256,8]{1,0:T(8,128)S(1)}, f32[256,8]{1,0:T(8,128)}, f32[2048,512]{1,0:T(8,128)}) %tuple.50, (s32[1,256]{1,0:T(1,128)S(1)}, s32[256]{0:T(256)S(1)}, s32[]{:T(128)}, s32[]{:T(128)}, ...), branch_computations={%region_3.3_spmd, %region_4.6_spmd} | conditional | flops 1147933184 | bytes 23436372 | solution.py:63
  578.4 5.7 multiply_add_fusion
  604.5 12.8 %collective-permute-done = bf16[1,256,1024]{2,1,0:T(8,128)(2,1)S(1)} collective-permute-done((bf16[1,256,1024]{2,1,0:T(8,128)(2,1)S(1)}, bf16[1,256,1024]{2,1,0:T(8,128)(2,1)S(1)}, u32[]{:S(2)}, u32[]{:S(2)}) %collective-permute-start) | collective-permute-done | bytes 524320 | tf_op jit(solution)/shard_map/ppermute | solution.py:11
  (488 shorter events, 265.4 us)
Async XLA Ops:
  6.5 596.7 %copy-start = (bf16[1,8,512,128]{3,2,1,0:T(8,128)(2,1)S(1)}, bf16[1,8,512,128]{3,2,1,0:T(8,128)(2,1)}, u32[]{:S(2)}) copy-start(bf16[1,8,512,128]{3,2,1,0:T(8,128)(2,1)} %param.13) | copy-start | bytes 3145732
  6.5 96.3 %all-gather.3.cloned.1.call-start = ((), (), s32[]{:S(2)}) async-start(), calls=%async_computation | async-start | bytes 9732096 | tf_op jit(solution)/shard_map/all_gather | solution.py:112
  7.3 5.5 copy-start.2
  7.3 38.4 %copy-start.3 = (s32[32,32]{1,0:T(8,128)S(1)}, s32[32,32]{1,0:T(8,128)}, u32[]{:S(2)}) copy-start(s32[32,32]{1,0:T(8,128)} %param.12) | copy-start | bytes 12292
  133.2 3.2 copy-start.1
  152.6 3.2 copy-start.1
  172.1 3.2 copy-start.1
  191.5 3.2 copy-start.1
  216.1 3.2 copy-start.1
  235.5 3.2 copy-start.1
  255.0 3.2 copy-start.1
  274.4 3.2 copy-start.1
  293.8 3.2 copy-start.1
  313.2 3.2 copy-start.1
  332.6 3.2 copy-start.1
  352.0 3.2 copy-start.1
  371.4 3.2 copy-start.1
  396.0 3.2 copy-start.1
  415.5 3.2 copy-start.1
  434.9 3.2 copy-start.1
  454.3 3.2 copy-start.1
  473.8 3.2 copy-start.1
  493.2 3.2 copy-start.1
  512.6 3.2 copy-start.1
  532.0 3.2 copy-start.1
  551.4 3.2 copy-start.1
  570.9 3.2 copy-start.1
  604.4 12.9 %collective-permute-start = (bf16[1,256,1024]{2,1,0:T(8,128)(2,1)S(1)}, bf16[1,256,1024]{2,1,0:T(8,128)(2,1)S(1)}, u32[]{:S(2)}, u32[]{:S(2)}) collective-permute-start(bf16[1,256,1024]{2,1,0:T(8,128)(2,1)S(1)} %copy.13), channel_id=1, source_target_pairs={{0,1},{1,2},{2,3},{3,4},{4,5},{5,6},{6,7},{7,0},{8,9},{9,10},{10,1... | collective-permute-start | bytes 1572872 | tf_op jit(solution)/shard_map/ppermute | solution.py:11
Sparse Core Ops, SparseCore 0:
  9.1 93.6 all-gather.2
where the time goes:
time: 630 us; the launch traced here: 625 us
  matrix products  205 us (33%)
  other arithmetic  121 us (19%)
  local copies, waits for them, and re-layouts  116 us (18%)
  waiting for transfers between devices  70 us (11%)
  loops' own time  65.6 us (10%)
  blocking collectives  32.8 us (5%)
  between operations  13.5 us (2%)
    dot_general x23, matrix products, compute(): lax.dot_general(weights_low, values, (((1,), (1,)), ((), ())), preferred_...  132 us
    dot_general x23, matrix products, compute(): jnp.dot(query_rows, cache_block, preferred_element_type=jnp.float32)  73 us
    another operation x1, loops' own time, shards(): lax.fori_loop(0, width_piece // step_size, over_steps, initial)  63.2 us
    all_gather x1, waiting for transfers between devices, shards(): cache_piece = lax.all_gather(latent_cache, 'ctx', axis=2, tiled=True)[0]  56.5 us
    reduce_sum x32, other arithmetic, attend_block(): jnp.sum(jnp.where(jnp.arange(table_row.shape[0], dtype=jnp.int32) == key_...  40.7 us
    add x23, other arithmetic, compute(): total_new = total_old * factor + jnp.sum(weights, axis=2)  38.1 us
    reduce_sum x23, other arithmetic, compute(): total_new = total_old * factor + jnp.sum(weights, axis=2)  35.3 us
    all_gather x1, blocking collectives, shards(): lax.all_gather(doc_ids[:, None, :], 'ctx', axis=2, tiled=True)[0, 0]  32.8 us
  transfers between devices with their start and end apart: 2, of which 2 were waited for; matrix products, arithmetic and copies ran while one was open for 1% of the time, Pallas kernels for 0%

commit v1 on v0

v1 whole, which is shorter than its diff:
```python
import functools
import jax
import jax.numpy as jnp
from jax import lax
from jax.experimental import pallas as pl
from jax.experimental.pallas import tpu as pltpu
from jax.sharding import PartitionSpec as P

very_low = -1e30
log2_e = 1.4426950408889634
id_rows = 16
documents = 8


def dot(a, b, of_a, of_b):
    return lax.dot_general(a, b, (((of_a,), (of_b,)), ((), ())), preferred_element_type=jnp.float32)


def attend(places, first, final, factor_scale, ids_s, table, ids_v, queries, *refs):
    count = len(places)
    blocks, refs = refs[:count], refs[count:]
    if final:
        up, refs = refs[0], refs[1:]
    if not first:
        refs = refs[3:]
    (peak, total, accum), refs = refs[:3], refs[3:]
    if final:
        out, refs = refs[0], refs[1:]
    flipped, values, bias, score_buf, weight_buf, factor_buf = refs
    heads, latent, tokens = accum.shape
    width = queries.shape[0] // heads
    me = lax.axis_index("ctx")
    if first:
        peak[...] = jnp.full(peak.shape, very_low, jnp.float32)
        total[...] = jnp.zeros(total.shape, jnp.float32)
        accum[...] = jnp.zeros(accum.shape, jnp.float32)
    weight_buf[1] = jnp.zeros(weight_buf.shape[1:], weight_buf.dtype)
    factor_buf[1] = jnp.ones(factor_buf.shape[1:], factor_buf.dtype)
    first_id = ids_s[0, 0]
    query_ids = ids_v[...]
    key_at = lax.broadcasted_iota(jnp.int32, (tokens, tokens), 0)
    live_count = jnp.int32(0)
    for j, (back, flip) in enumerate(places):
        block = blocks[j]
        origin = (me ^ flip) - 4 * back
        key_ids = block[width : width + id_rows, :].astype(jnp.float32)[0:1, :]
        before = jnp.sum(jnp.where(key_ids < first_id.astype(jnp.float32), 1.0, 0.0)).astype(jnp.int32)
        if back == 0 and flip == 0:
            live = jnp.bool_(True)
        else:
            hit = table[me, jnp.maximum(origin, 0)]
            live = (origin >= 0) & (origin < me) & (hit == 1) & (before < tokens)

        def pack(block=block, key_ids=key_ids, before=before, slot=live_count, own=back == 0 and flip == 0):
            flipped[slot] = block[0:width, :].T
            values[slot] = block[0:latent, :]
            if own:
                start = jnp.zeros(query_ids.shape, jnp.int32)
                for d in range(documents):
                    below = jnp.sum(jnp.where(key_ids < float(d), 1.0, 0.0), axis=1, keepdims=True)
                    start = jnp.where(query_ids == d, below.astype(jnp.int32), start)
                query_at = lax.broadcasted_iota(jnp.int32, (tokens, tokens), 1)
                allowed = (key_at >= start) & (key_at <= query_at)
            else:
                allowed = (key_at >= before) & (query_ids == first_id)
            bias[slot] = jnp.where(allowed, 0.0, very_low)

        if back == 0 and flip == 0:
            pack()
        else:
            pl.when(live)(pack)
        live_count = live_count + live.astype(jnp.int32)

    def score(slot, head, half):
        rows = queries[head * width : (head + 1) * width, :]
        score_buf[half] = dot(flipped[slot], rows, 1, 0) + bias[slot]

    def weigh(head, half):
        scores = score_buf[half]
        old = peak[head : head + 1, :]
        new = jnp.maximum(old, jnp.max(scores, axis=0, keepdims=True))
        factor = jnp.exp2((old - new) * factor_scale)
        weights = jnp.exp2((scores - new) * factor_scale)
        total[head : head + 1, :] = total[head : head + 1, :] * factor + jnp.sum(weights, axis=0, keepdims=True)
        peak[head : head + 1, :] = new
        factor_buf[half] = jnp.broadcast_to(factor, factor_buf.shape[1:])
        weight_buf[half] = weights.astype(jnp.bfloat16)

    def mix(slot, head, half):
        accum[head] = accum[head] * factor_buf[half][0:1, :] + dot(values[slot], weight_buf[half], 1, 0)

    @pl.when(live_count > 0)
    def _():
        score(0, 0, 0)

        def over_live(slot, carry):
            after, prior = jnp.minimum(slot + 1, live_count - 1), jnp.maximum(slot - 1, 0)
            for head in range(heads):
                half = head % 2
                score(slot if head < heads - 1 else after, (head + 1) % heads, 1 - half)
                weigh(head, half)
                mix(slot if head > 0 else prior, (head - 1) % heads, 1 - half)
            return carry

        lax.fori_loop(0, live_count, over_live, 0)
        mix(live_count - 1, heads - 1, (heads - 1) % 2)

    if final:
        value_width = up.shape[2]
        for head in range(heads):
            mixed = (accum[head] / total[head : head + 1, :]).astype(jnp.bfloat16)
            part = dot(up[head], mixed, 0, 0)
            out[:, head * value_width : (head + 1) * value_width] = part.T.astype(jnp.bfloat16)


def stage(places, blocks, ids, table, queries, state, up, sizes):
    heads, latent, tokens, width, value_width = sizes
    first, final = state is None, up is not None
    count = len(places)
    scalars, vectors = pl.BlockSpec(memory_space=pltpu.SMEM), pl.BlockSpec(memory_space=pltpu.VMEM)
    shapes = [((heads, tokens), jnp.float32), ((heads, tokens), jnp.float32), ((heads, latent, tokens), jnp.float32)]
    operands = [ids, table, ids, queries, *blocks]
    specs = [scalars, scalars, vectors, vectors] + [vectors] * count
    aliases = {}
    if final:
        operands.append(up)
        specs.append(vectors)
    out_shape = [pltpu.VMEM(shape, dtype) for shape, dtype in shapes]
    if final:
        out_shape.append(jax.ShapeDtypeStruct((tokens, heads * value_width), jnp.bfloat16))
    if not first:
        aliases = {len(operands) + i: i for i in range(3)}
        operands += [pltpu.with_memory_space_constraint(x, pltpu.VMEM) for x in state]
        specs += [vectors] * 3
    scratch = [
        pltpu.VMEM((count, tokens, width), jnp.bfloat16),
        pltpu.VMEM((count, latent, tokens), jnp.bfloat16),
        pltpu.VMEM((count, tokens, tokens), jnp.float32),
        pltpu.VMEM((2, tokens, tokens), jnp.float32),
        pltpu.VMEM((2, tokens, tokens), jnp.bfloat16),
        pltpu.VMEM((2, 8, tokens), jnp.float32),
    ]
    scale = (value_width + width - latent) ** -0.5 * log2_e
    work = 2 * count * heads * tokens * tokens * (width + latent)
    result = pl.pallas_call(
        functools.partial(attend, tuple(places), first, final, scale),
        out_shape=out_shape,
        in_specs=specs,
        out_specs=[vectors] * len(out_shape),
        scratch_shapes=scratch,
        input_output_aliases=aliases,
        cost_estimate=pl.CostEstimate(
            flops=work, bytes_accessed=count * 2 * width * tokens, transcendentals=count * heads * tokens * tokens
        ),
        compiler_params=pltpu.CompilerParams(vmem_limit_bytes=24 * 2**20),
        name="attend",
    )(*operands)
    return result[3] if final else result


def shards(queries, latent_cache, doc_ids, block_table, w_uv):
    tokens, heads, latent, value_width = queries.shape[1], w_uv.shape[1], w_uv.shape[2], w_uv.shape[3]
    width = latent_cache.shape[1]
    sizes = (heads, latent, tokens, width, value_width)
    devices = lax.axis_size("ctx")
    planes = devices // 4

    def send(x, to, least=0):
        pairs = [(i, to(i)) for i in range(devices)]
        return lax.ppermute(x, "ctx", [(i, o) for i, o in pairs if least <= o // 4 and 0 <= o < devices])

    across = lambda x, least=0: send(x, lambda i: i ^ 2, least)
    core = lambda x, least=0: send(x, lambda i: i ^ 1, least)
    up_one = lambda x, least: send(x, lambda i: i + 4, least)

    ids = jnp.broadcast_to(doc_ids.astype(jnp.bfloat16), (id_rows, tokens))
    own = jnp.concatenate([latent_cache[0], ids], axis=0)
    turned = queries[0].T
    queries_t = pltpu.with_memory_space_constraint(turned, pltpu.VMEM)

    def run(places, blocks, state, up=None):
        return stage(places, blocks, doc_ids, block_table, queries_t, state, up, sizes)

    ups, far = {0: own}, {}
    across_of, core_of, core_across_of = {}, {}, {}
    core_of[0], across_of[0] = core(own), across(own)
    ups[1] = up_one(own, 1)
    ups[6] = send(own, lambda i: i + 24)
    ups[5] = send(own, lambda i: i + 20)
    state = run([(0, 0), (0, 1)], [own, core_of[0]], None)
    for k in (1, 2, 3, 4):
        if k < 4:
            ups[k + 1] = up_one(ups[k], k + 1)
        across_of[k], core_of[k] = across(ups[k], k), core(ups[k], k)
        core_across_of[k - 1] = core(across_of[k - 1], k - 1)
        places = [(k - 1, 2), (k - 1, 3), (k, 0), (k, 1)]
        blocks = [across_of[k - 1], core_across_of[k - 1], ups[k], core_of[k]]
        if k == 4:
            for far in (5, 6):
                core_of[far], across_of[far] = core(ups[far], far), across(ups[far], far)
                places += [(far, 0), (far, 1)]
                blocks += [ups[far], core_of[far]]
        state = run(places, blocks, state)
    places, blocks = [], []
    for k in (4, 5, 6):
        core_across_of[k] = core(across_of[k], k)
        places += [(k, 2), (k, 3)]
        blocks += [across_of[k], core_across_of[k]]
    heads_out = run(places, blocks, state, w_uv[0])
    sections = lax.axis_size("section")
    return lax.ppermute(heads_out[None], "section", [(i, (i + 1) % sections) for i in range(sections)])


def solution(mesh):
    placed = (
        P("section", "ctx", None),
        P("section", None, "ctx"),
        P("section", "ctx"),
        P(),
        P("section", None, None, None),
    )
    return jax.shard_map(
        shards, mesh=mesh, in_specs=placed, out_specs=P("section", "ctx", None), check_vma=False
    )
```

time: 630 us -> 154 us (0.24)
  the two profiles are of different devices: /device:TPU:224 before, /device:TPU:194 now
where the time goes in v1:
time: 154 us; the launch traced here: 151 us
  starting transfers between devices  61.3 us (40%)
  Pallas kernels  45.7 us (30%)
  waiting for transfers between devices  36.9 us (24%)
  local copies, waits for them, and re-layouts  5.32 us (3%)
  other arithmetic  1.75 us (1%)
    ppermute x27, starting transfers between devices, send(): lax.ppermute(x, 'ctx', [(i, o) for i, o in pairs if least <= o // 4 and 0...  61 us
    pallas_call x6, Pallas kernels, stage(): pl.pallas_call(functools.partial(attend, tuple(places), first, final, sca...  45.7 us
    ppermute x27, waiting for transfers between devices, send(): lax.ppermute(x, 'ctx', [(i, o) for i, o in pairs if least <= o // 4 and 0...  19.5 us
    ppermute x1, waiting for transfers between devices, shards(): lax.ppermute(heads_out[None], 'section', [(i, (i + 1) % sections) for i i...  17.5 us
    unnamed x12, local copies, waits for them, and re-layouts  5.31 us
  transfers between devices with their start and end apart: 28, of which 4 were waited for; matrix products, arithmetic and copies ran while one was open for 2% of the time, Pallas kernels for 24%

profile of v1, /device:TPU:194, one launch (start us, length us, event | category | flops | bytes accessed | tf_op | source)
XLA Modules:
  0.0 151.5 jit_solution(3572530492549151844)
XLA Ops:
  0.0 0.8 convert_reduce_fusion
  0.8 1.0 pad_maximum_fusion.refs_0_
  1.8 2.9 %collective-permute-start = (bf16[592,256]{1,0:T(8,128)(2,1)S(1)}, bf16[592,256]{1,0:T(8,128)(2,1)}, u32[]{:S(2)}, u32[]{:S(2)}) collective-permute-start(bf16[592,256]{1,0:T(8,128)(2,1)S(1)} %pad_maximum_fusion.refs_0_), channel_id=1, source_target_pairs={{0,32},{8,40},{16,48},{24,56},{32,64},{40,72},{48,80},{56,88},{64,... | collective-permute-start | bytes 909320 | tf_op jit(solution)/shard_map/ppermute | solution.py:170
  4.7 0.1 collective-permute-start.26
  4.8 0.6 collective-permute-start.23
  5.4 1.3 collective-permute-start.6
  6.7 1.3 collective-permute-start.9
  8.0 4.7 %collective-permute-done.refs_2_ = bf16[592,256]{1,0:T(8,128)(2,1)} collective-permute-done((bf16[592,256]{1,0:T(8,128)(2,1)S(1)}, bf16[592,256]{1,0:T(8,128)(2,1)}, u32[]{:S(2)}, u32[]{:S(2)}) %collective-permute-start) | collective-permute-done | bytes 303136 | tf_op jit(solution)/shard_map/ppermute | solution.py:170
  12.7 2.9 %collective-permute-start.1 = (bf16[592,256]{1,0:T(8,128)(2,1)}, bf16[592,256]{1,0:T(8,128)(2,1)}, u32[]{:S(2)}, u32[]{:S(2)}) collective-permute-start(bf16[592,256]{1,0:T(8,128)(2,1)} %collective-permute-done.refs_2_), channel_id=1, source_target_pairs={{32,64},{40,72},{48,80},{56,88},{64,96},{72,104},{80,112},{88,120}... | collective-permute-start | bytes 909320 | tf_op jit(solution)/shard_map/ppermute | solution.py:170
  15.6 0.0 collective-permute-done.26.refs_1_
  15.6 0.0 copy-start.1
  15.6 0.7 copy-done.1
  16.3 1.9 %collective-permute-start.25 = (bf16[592,256]{1,0:T(8,128)(2,1)}, bf16[592,256]{1,0:T(8,128)(2,1)}, u32[]{:S(2)}, u32[]{:S(2)}) collective-permute-start(bf16[592,256]{1,0:T(8,128)(2,1)} %collective-permute-done.refs_2_), channel_id=1, source_target_pairs={{32,40},{40,32},{48,56},{56,48},{64,72},{72,64},{80,88},{88,80},{9... | collective-permute-start | bytes 909320 | tf_op jit(solution)/shard_map/ppermute | solution.py:170
  18.3 0.0 collective-permute-done.23.refs_0_
  18.3 0.6 collective-permute-start.24
  18.9 6.2 %collective-permute-done.6.refs_4_ = bf16[592,256]{1,0:T(8,128)(2,1)S(1)} collective-permute-done((bf16[592,256]{1,0:T(8,128)(2,1)S(1)}, bf16[592,256]{1,0:T(8,128)(2,1)S(1)}, u32[]{:S(2)}, u32[]{:S(2)}) %collective-permute-start.6) | collective-permute-done | bytes 303136 | tf_op jit(solution)/shard_map/ppermute | solution.py:170
  25.0 3.4 %collective-permute-start.20 = (bf16[592,256]{1,0:T(8,128)(2,1)}, bf16[592,256]{1,0:T(8,128)(2,1)}, u32[]{:S(2)}, u32[]{:S(2)}) collective-permute-start(bf16[592,256]{1,0:T(8,128)(2,1)} %collective-permute-done.refs_2_), channel_id=1, source_target_pairs={{32,48},{40,56},{48,32},{56,40},{64,80},{72,88},{80,64},{88,72},{9... | collective-permute-start | bytes 909320 | tf_op jit(solution)/shard_map/ppermute | solution.py:170
  28.4 2.8 %copy.21 = bf16[1,256,4608]{1,2,0:T(8,128)(2,1)S(1)} copy(bf16[1,256,4608]{2,1,0:T(8,128)(2,1)} %param.5) | data formatting | bytes 4718592 | tf_op args[0]
  31.3 0.0 copy-start.2
  31.3 1.0 copy-done.2
  32.3 3.5 %attend.6 = (f32[8,256]{1,0:T(8,128)S(1)}, f32[8,256]{1,0:T(8,128)S(1)}, f32[8,512,256]{2,1,0:T(8,128)S(1)}) custom-call(s32[1,256]{1,0:T(1,128)S(1)} %copy-done.4, s32[32,32]{1,0:T(8,128)S(1)} %copy-done.3, s32[1,256]{1,0:T(1,128)S(1)} %copy-done.4, bf16[4608,256]{1,0:T(8,128)(2,1)S(1)} %bitcast.6, bf16[592,256]{1,0:T(8,128)(2,1)S(1)} %pad_maximum_fusion.refs_0_, ...), custom_call_target="tpu_custom_call" | custom-call | flops 2281701376 | bytes 589824 | tf_op jit(solution)/shard_map/attend/pallas_call | solution.py:145
  35.8 8.6 %collective-permute-done.9.refs_6_ = bf16[592,256]{1,0:T(8,128)(2,1)S(1)} collective-permute-done((bf16[592,256]{1,0:T(8,128)(2,1)S(1)}, bf16[592,256]{1,0:T(8,128)(2,1)S(1)}, u32[]{:S(2)}, u32[]{:S(2)}) %collective-permute-start.9) | collective-permute-done | bytes 303136 | tf_op jit(solution)/shard_map/ppermute | solution.py:170
  44.3 1.9 %collective-permute-start.15 = (bf16[592,256]{1,0:T(8,128)(2,1)S(1)}, bf16[592,256]{1,0:T(8,128)(2,1)S(1)}, u32[]{:S(2)}, u32[]{:S(2)}) collective-permute-start(bf16[592,256]{1,0:T(8,128)(2,1)S(1)} %collective-permute-done.6.refs_4_), channel_id=1, source_target_pairs={{160,168},{168,160},{176,184},{184,176},{192,200},{200,192},{208,2... | collective-permute-start | bytes 909320 | tf_op jit(solution)/shard_map/ppermute | solution.py:170
  46.3 0.0 collective-permute-done.1.refs_2_
  46.3 2.4 %collective-permute-start.22 = (bf16[592,256]{1,0:T(8,128)(2,1)}, bf16[592,256]{1,0:T(8,128)(2,1)S(1)}, u32[]{:S(2)}, u32[]{:S(2)}) collective-permute-start(bf16[592,256]{1,0:T(8,128)(2,1)} %collective-permute-done.1.refs_2_), channel_id=1, source_target_pairs={{64,72},{72,64},{80,88},{88,80},{96,104},{104,96},{112,120},{120,1... | collective-permute-start | bytes 909320 | tf_op jit(solution)/shard_map/ppermute | solution.py:170
  48.7 0.0 collective-permute-done.25.refs_3_
  48.7 1.9 %collective-permute-start.2 = (bf16[592,256]{1,0:T(8,128)(2,1)}, bf16[592,256]{1,0:T(8,128)(2,1)S(1)}, u32[]{:S(2)}, u32[]{:S(2)}) collective-permute-start(bf16[592,256]{1,0:T(8,128)(2,1)} %collective-permute-done.1.refs_2_), channel_id=1, source_target_pairs={{64,96},{72,104},{80,112},{88,120},{96,128},{104,136},{112,144},{1... | collective-permute-start | bytes 909320 | tf_op jit(solution)/shard_map/ppermute | solution.py:170
  50.6 3.4 %collective-permute-start.17 = (bf16[592,256]{1,0:T(8,128)(2,1)}, bf16[592,256]{1,0:T(8,128)(2,1)S(1)}, u32[]{:S(2)}, u32[]{:S(2)}) collective-permute-start(bf16[592,256]{1,0:T(8,128)(2,1)} %collective-permute-done.1.refs_2_), channel_id=1, source_target_pairs={{64,80},{72,88},{80,64},{88,72},{96,112},{104,120},{112,96},{120,1... | collective-permute-start | bytes 909320 | tf_op jit(solution)/shard_map/ppermute | solution.py:170
  54.0 0.0 collective-permute-done.20.refs_0_
  54.1 1.9 %collective-permute-start.21 = (bf16[592,256]{1,0:T(8,128)(2,1)}, bf16[592,256]{1,0:T(8,128)(2,1)S(1)}, u32[]{:S(2)}, u32[]{:S(2)}) collective-permute-start(bf16[592,256]{1,0:T(8,128)(2,1)} %collective-permute-done.20.refs_0_), channel_id=1, source_target_pairs={{32,40},{40,32},{48,56},{56,48},{64,72},{72,64},{80,88},{88,80},{9... | collective-permute-start | bytes 909320 | tf_op jit(solution)/shard_map/ppermute | solution.py:170
  56.0 6.1 %attend.7 = (f32[8,256]{1,0:T(8,128)S(1)}, f32[8,256]{1,0:T(8,128)S(1)}, f32[8,512,256]{2,1,0:T(8,128)S(1)}) custom-call(s32[1,256]{1,0:T(1,128)S(1)} %copy-done.4, s32[32,32]{1,0:T(8,128)S(1)} %copy-done.3, s32[1,256]{1,0:T(1,128)S(1)} %copy-done.4, bf16[4608,256]{1,0:T(8,128)(2,1)S(1)} %bitcast.7, ...), custom_call_target="tpu_custom_call", output_to_operand_aliasing={{0}: (8, {}), {1}: (9, {}), {2}: (10, {})} | custom-call | flops 4563402752 | bytes 1179648 | tf_op jit(solution)/shard_map/attend/pallas_call | solution.py:145
  62.1 4.3 %collective-permute-start.16 = (bf16[592,256]{1,0:T(8,128)(2,1)S(1)}, bf16[592,256]{1,0:T(8,128)(2,1)S(1)}, u32[]{:S(2)}, u32[]{:S(2)}) collective-permute-start(bf16[592,256]{1,0:T(8,128)(2,1)S(1)} %collective-permute-done.9.refs_6_), channel_id=1, source_target_pairs={{192,200},{200,192},{208,216},{216,208},{224,232},{232,224},{240,2... | collective-permute-start | bytes 909320 | tf_op jit(solution)/shard_map/ppermute | solution.py:170
  66.4 0.0 collective-permute-done.2.refs_2_
  66.4 1.9 %collective-permute-start.19 = (bf16[592,256]{1,0:T(8,128)(2,1)S(1)}, bf16[592,256]{1,0:T(8,128)(2,1)S(1)}, u32[]{:S(2)}, u32[]{:S(2)}) collective-permute-start(bf16[592,256]{1,0:T(8,128)(2,1)S(1)} %collective-permute-done.2.refs_2_), channel_id=1, source_target_pairs={{96,104},{104,96},{112,120},{120,112},{128,136},{136,128},{144,152... | collective-permute-start | bytes 909320 | tf_op jit(solution)/shard_map/ppermute | solution.py:170
  68.4 1.9 %collective-permute-start.3 = (bf16[592,256]{1,0:T(8,128)(2,1)S(1)}, bf16[592,256]{1,0:T(8,128)(2,1)S(1)}, u32[]{:S(2)}, u32[]{:S(2)}) collective-permute-start(bf16[592,256]{1,0:T(8,128)(2,1)S(1)} %collective-permute-done.2.refs_2_), channel_id=1, source_target_pairs={{96,128},{104,136},{112,144},{120,152},{128,160},{136,168},{144,17... | collective-permute-start | bytes 909320 | tf_op jit(solution)/shard_map/ppermute | solution.py:170
  70.3 0.0 collective-permute-done.21.refs_1_
  70.3 1.9 %collective-permute-start.12 = (bf16[592,256]{1,0:T(8,128)(2,1)S(1)}, bf16[592,256]{1,0:T(8,128)(2,1)S(1)}, u32[]{:S(2)}, u32[]{:S(2)}) collective-permute-start(bf16[592,256]{1,0:T(8,128)(2,1)S(1)} %collective-permute-done.2.refs_2_), channel_id=1, source_target_pairs={{96,112},{104,120},{112,96},{120,104},{128,144},{136,152},{144,128... | collective-permute-start | bytes 909320 | tf_op jit(solution)/shard_map/ppermute | solution.py:170
  72.2 0.0 collective-permute-done.17.refs_0_
  72.3 2.4 %collective-permute-start.18 = (bf16[592,256]{1,0:T(8,128)(2,1)S(1)}, bf16[592,256]{1,0:T(8,128)(2,1)S(1)}, u32[]{:S(2)}, u32[]{:S(2)}) collective-permute-start(bf16[592,256]{1,0:T(8,128)(2,1)S(1)} %collective-permute-done.17.refs_0_), channel_id=1, source_target_pairs={{64,72},{72,64},{80,88},{88,80},{96,104},{104,96},{112,120},{120,1... | collective-permute-start | bytes 909320 | tf_op jit(solution)/shard_map/ppermute | solution.py:170
  74.7 7.8 %attend.8 = (f32[8,256]{1,0:T(8,128)S(1)}, f32[8,256]{1,0:T(8,128)S(1)}, f32[8,512,256]{2,1,0:T(8,128)S(1)}) custom-call(s32[1,256]{1,0:T(1,128)S(1)} %copy-done.4, s32[32,32]{1,0:T(8,128)S(1)} %copy-done.3, s32[1,256]{1,0:T(1,128)S(1)} %copy-done.4, bf16[4608,256]{1,0:T(8,128)(2,1)S(1)} %bitcast.8, ...), custom_call_target="tpu_custom_call", output_to_operand_aliasing={{0}: (8, {}), {1}: (9, {}), {2}: (10, {})} | custom-call | flops 4563402752 | bytes 1179648 | tf_op jit(solution)/shard_map/attend/pallas_call | solution.py:145
  82.5 0.0 collective-permute-done.16.refs_7_
  82.5 5.6 %collective-permute-start.10 = (bf16[592,256]{1,0:T(8,128)(2,1)S(1)}, bf16[592,256]{1,0:T(8,128)(2,1)S(1)}, u32[]{:S(2)}, u32[]{:S(2)}) collective-permute-start(bf16[592,256]{1,0:T(8,128)(2,1)S(1)} %collective-permute-done.9.refs_6_), channel_id=1, source_target_pairs={{192,208},{200,216},{208,192},{216,200},{224,240},{232,248},{240,2... | collective-permute-start | bytes 909320 | tf_op jit(solution)/shard_map/ppermute | solution.py:170
  88.1 1.9 %collective-permute-start.7 = (bf16[592,256]{1,0:T(8,128)(2,1)S(1)}, bf16[592,256]{1,0:T(8,128)(2,1)S(1)}, u32[]{:S(2)}, u32[]{:S(2)}) collective-permute-start(bf16[592,256]{1,0:T(8,128)(2,1)S(1)} %collective-permute-done.6.refs_4_), channel_id=1, source_target_pairs={{160,176},{168,184},{176,160},{184,168},{192,208},{200,216},{208,1... | collective-permute-start | bytes 909320 | tf_op jit(solution)/shard_map/ppermute | solution.py:170
  90.0 0.0 collective-permute-done.3.refs_2_
  90.0 1.9 %collective-permute-start.14 = (bf16[592,256]{1,0:T(8,128)(2,1)S(1)}, bf16[592,256]{1,0:T(8,128)(2,1)S(1)}, u32[]{:S(2)}, u32[]{:S(2)}) collective-permute-start(bf16[592,256]{1,0:T(8,128)(2,1)S(1)} %collective-permute-done.3.refs_2_), channel_id=1, source_target_pairs={{128,136},{136,128},{144,152},{152,144},{160,168},{168,160},{176,1... | collective-permute-start | bytes 909320 | tf_op jit(solution)/shard_map/ppermute | solution.py:170
  92.0 0.0 collective-permute-done.18.refs_1_
  92.0 3.9 %collective-permute-start.4 = (bf16[592,256]{1,0:T(8,128)(2,1)S(1)}, bf16[592,256]{1,0:T(8,128)(2,1)S(1)}, u32[]{:S(2)}, u32[]{:S(2)}) collective-permute-start(bf16[592,256]{1,0:T(8,128)(2,1)S(1)} %collective-permute-done.3.refs_2_), channel_id=1, source_target_pairs={{128,144},{136,152},{144,128},{152,136},{160,176},{168,184},{176,1... | collective-permute-start | bytes 909320 | tf_op jit(solution)/shard_map/ppermute | solution.py:170
  95.9 2.1 %collective-permute-start.13 = (bf16[592,256]{1,0:T(8,128)(2,1)S(1)}, bf16[592,256]{1,0:T(8,128)(2,1)S(1)}, u32[]{:S(2)}, u32[]{:S(2)}) collective-permute-start(bf16[592,256]{1,0:T(8,128)(2,1)S(1)} %collective-permute-done.12.refs_0_), channel_id=1, source_target_pairs={{96,104},{104,96},{112,120},{120,112},{128,136},{136,128},{144,152... | collective-permute-start | bytes 909320 | tf_op jit(solution)/shard_map/ppermute | solution.py:170
  98.0 5.8 %attend.9 = (f32[8,256]{1,0:T(8,128)S(1)}, f32[8,256]{1,0:T(8,128)S(1)}, f32[8,512,256]{2,1,0:T(8,128)S(1)}) custom-call(s32[1,256]{1,0:T(1,128)S(1)} %copy-done.4, s32[32,32]{1,0:T(8,128)S(1)} %copy-done.3, s32[1,256]{1,0:T(1,128)S(1)} %copy-done.4, bf16[4608,256]{1,0:T(8,128)(2,1)S(1)} %bitcast.9, ...), custom_call_target="tpu_custom_call", output_to_operand_aliasing={{0}: (8, {}), {1}: (9, {}), {2}: (10, {})} | custom-call | flops 4563402752 | bytes 1179648 | tf_op jit(solution)/shard_map/attend/pallas_call | solution.py:145
  103.9 0.0 collective-permute-done.10.refs_4_
  103.9 2.2 %collective-permute-start.11 = (bf16[592,256]{1,0:T(8,128)(2,1)S(1)}, bf16[592,256]{1,0:T(8,128)(2,1)S(1)}, u32[]{:S(2)}, u32[]{:S(2)}) collective-permute-start(bf16[592,256]{1,0:T(8,128)(2,1)S(1)} %collective-permute-done.10.refs_4_), channel_id=1, source_target_pairs={{192,200},{200,192},{208,216},{216,208},{224,232},{232,224},{240,2... | collective-permute-start | bytes 909320 | tf_op jit(solution)/shard_map/ppermute | solution.py:170
  106.1 2.1 %collective-permute-start.8 = (bf16[592,256]{1,0:T(8,128)(2,1)S(1)}, bf16[592,256]{1,0:T(8,128)(2,1)S(1)}, u32[]{:S(2)}, u32[]{:S(2)}) collective-permute-start(bf16[592,256]{1,0:T(8,128)(2,1)S(1)} %collective-permute-done.7.refs_2_), channel_id=1, source_target_pairs={{160,168},{168,160},{176,184},{184,176},{192,200},{200,192},{208,2... | collective-permute-start | bytes 909320 | tf_op jit(solution)/shard_map/ppermute | solution.py:170
  108.2 0.0 collective-permute-done.4.refs_0_
  108.3 2.2 %collective-permute-start.5 = (bf16[592,256]{1,0:T(8,128)(2,1)S(1)}, bf16[592,256]{1,0:T(8,128)(2,1)S(1)}, u32[]{:S(2)}, u32[]{:S(2)}) collective-permute-start(bf16[592,256]{1,0:T(8,128)(2,1)S(1)} %collective-permute-done.4.refs_0_), channel_id=1, source_target_pairs={{128,136},{136,128},{144,152},{152,144},{160,168},{168,160},{176,1... | collective-permute-start | bytes 909320 | tf_op jit(solution)/shard_map/ppermute | solution.py:170
  110.5 0.0 collective-permute-done.14.refs_3_
  110.5 0.0 collective-permute-done.13.refs_1_
  110.5 0.0 copy-start
  110.5 13.8 %attend.10 = (f32[8,256]{1,0:T(8,128)S(1)}, f32[8,256]{1,0:T(8,128)S(1)}, f32[8,512,256]{2,1,0:T(8,128)S(1)}) custom-call(s32[1,256]{1,0:T(1,128)S(1)} %copy-done.4, s32[32,32]{1,0:T(8,128)S(1)} %copy-done.3, s32[1,256]{1,0:T(1,128)S(1)} %copy-done.4, bf16[4608,256]{1,0:T(8,128)(2,1)S(1)} %bitcast.10, ...), custom_call_target="tpu_custom_call", output_to_operand_aliasing={{0}: (12, {}), {1}: (13, {}), {2}: (14, {})} | custom-call | flops 9126805504 | bytes 2359296 | tf_op jit(solution)/shard_map/attend/pallas_call | solution.py:145
  124.3 0.0 collective-permute-done.11.refs_5_
  124.4 0.0 collective-permute-done.5.refs_1_
  124.4 8.5 %attend.11 = (f32[8,256]{1,0:T(8,128)S(1)}, f32[8,256]{1,0:T(8,128)S(1)}, f32[8,512,256]{2,1,0:T(8,128)S(1)}, bf16[256,1024]{1,0:T(8,128)(2,1)S(1)}) custom-call(s32[1,256]{1,0:T(1,128)S(1)} %copy-done.4, s32[32,32]{1,0:T(8,128)S(1)} %copy-done.3, s32[1,256]{1,0:T(1,128)S(1)} %copy-done.4, ...), custom_call_target="tpu_custom_call", output_to_operand_aliasing={{0}: (11, {}), {1}: (12, {}), {2}: (13, {})} | custom-call | flops 6845104128 | bytes 1769472 | tf_op jit(solution)/shard_map/attend/pallas_call | solution.py:145
  132.9 0.3 collective-permute-start.27
  133.2 17.5 %collective-permute-done.27 = bf16[1,256,1024]{2,1,0:T(8,128)(2,1)S(1)} collective-permute-done((bf16[1,256,1024]{2,1,0:T(8,128)(2,1)S(1)}, bf16[1,256,1024]{2,1,0:T(8,128)(2,1)S(1)}, u32[]{:S(2)}, u32[]{:S(2)}) %collective-permute-start.27) | collective-permute-done | bytes 524320 | tf_op jit(solution)/shard_map/ppermute | solution.py:211
  150.7 0.8 copy.38
  (13 shorter events, 0.0 us)
Async XLA Ops:
  0.0 31.3 %copy-start.4 = (s32[1,256]{1,0:T(1,128)S(1)}, s32[1,256]{1,0:T(1,128)}, u32[]{:S(2)}) copy-start(s32[1,256]{1,0:T(1,128)} %ids_v.11) | copy-start | bytes 3076
  0.0 31.3 %copy-start.3 = (s32[32,32]{1,0:T(8,128)S(1)}, s32[32,32]{1,0:T(8,128)}, u32[]{:S(2)}) copy-start(s32[32,32]{1,0:T(8,128)} %table.11) | copy-start | bytes 12292
  1.8 10.9 %collective-permute-start = (bf16[592,256]{1,0:T(8,128)(2,1)S(1)}, bf16[592,256]{1,0:T(8,128)(2,1)}, u32[]{:S(2)}, u32[]{:S(2)}) collective-permute-start(bf16[592,256]{1,0:T(8,128)(2,1)S(1)} %pad_maximum_fusion.refs_0_), channel_id=1, source_target_pairs={{0,32},{8,40},{16,48},{24,56},{32,64},{40,72},{48,80},{56,88},{64,... | collective-permute-start | bytes 909320 | tf_op jit(solution)/shard_map/ppermute | solution.py:170
  4.7 10.9 %collective-permute-start.26 = (bf16[592,256]{1,0:T(8,128)(2,1)S(1)}, bf16[592,256]{1,0:T(8,128)(2,1)S(1)}, u32[]{:S(2)}, u32[]{:S(2)}) collective-permute-start(bf16[592,256]{1,0:T(8,128)(2,1)S(1)} %pad_maximum_fusion.refs_0_), channel_id=1, source_target_pairs={{0,8},{8,0},{16,24},{24,16},{32,40},{40,32},{48,56},{56,48},{64,72... | collective-permute-start | bytes 909320 | tf_op jit(solution)/shard_map/ppermute | solution.py:170
  4.8 13.5 %collective-permute-start.23 = (bf16[592,256]{1,0:T(8,128)(2,1)S(1)}, bf16[592,256]{1,0:T(8,128)(2,1)}, u32[]{:S(2)}, u32[]{:S(2)}) collective-permute-start(bf16[592,256]{1,0:T(8,128)(2,1)S(1)} %pad_maximum_fusion.refs_0_), channel_id=1, source_target_pairs={{0,16},{8,24},{16,0},{24,8},{32,48},{40,56},{48,32},{56,40},{64,80... | collective-permute-start | bytes 909320 | tf_op jit(solution)/shard_map/ppermute | solution.py:170
  5.4 19.6 %collective-permute-start.6 = (bf16[592,256]{1,0:T(8,128)(2,1)S(1)}, bf16[592,256]{1,0:T(8,128)(2,1)S(1)}, u32[]{:S(2)}, u32[]{:S(2)}) collective-permute-start(bf16[592,256]{1,0:T(8,128)(2,1)S(1)} %pad_maximum_fusion.refs_0_), channel_id=1, source_target_pairs={{0,160},{8,168},{16,176},{24,184},{32,192},{40,200},{48,208},{56,2... | collective-permute-start | bytes 909320 | tf_op jit(solution)/shard_map/ppermute | solution.py:170
  6.7 37.6 %collective-permute-start.9 = (bf16[592,256]{1,0:T(8,128)(2,1)S(1)}, bf16[592,256]{1,0:T(8,128)(2,1)S(1)}, u32[]{:S(2)}, u32[]{:S(2)}) collective-permute-start(bf16[592,256]{1,0:T(8,128)(2,1)S(1)} %pad_maximum_fusion.refs_0_), channel_id=1, source_target_pairs={{0,192},{8,200},{16,208},{24,216},{32,224},{40,232},{48,240},{56,2... | collective-permute-start | bytes 909320 | tf_op jit(solution)/shard_map/ppermute | solution.py:170
  12.7 33.6 %collective-permute-start.1 = (bf16[592,256]{1,0:T(8,128)(2,1)}, bf16[592,256]{1,0:T(8,128)(2,1)}, u32[]{:S(2)}, u32[]{:S(2)}) collective-permute-start(bf16[592,256]{1,0:T(8,128)(2,1)} %collective-permute-done.refs_2_), channel_id=1, source_target_pairs={{32,64},{40,72},{48,80},{56,88},{64,96},{72,104},{80,112},{88,120}... | collective-permute-start | bytes 909320 | tf_op jit(solution)/shard_map/ppermute | solution.py:170
  15.6 0.7 copy-start.1
  16.3 32.4 %collective-permute-start.25 = (bf16[592,256]{1,0:T(8,128)(2,1)}, bf16[592,256]{1,0:T(8,128)(2,1)}, u32[]{:S(2)}, u32[]{:S(2)}) collective-permute-start(bf16[592,256]{1,0:T(8,128)(2,1)} %collective-permute-done.refs_2_), channel_id=1, source_target_pairs={{32,40},{40,32},{48,56},{56,48},{64,72},{72,64},{80,88},{88,80},{9... | collective-permute-start | bytes 909320 | tf_op jit(solution)/shard_map/ppermute | solution.py:170
  18.3 32.4 %collective-permute-start.24 = (bf16[592,256]{1,0:T(8,128)(2,1)}, bf16[592,256]{1,0:T(8,128)(2,1)}, u32[]{:S(2)}, u32[]{:S(2)}) collective-permute-start(bf16[592,256]{1,0:T(8,128)(2,1)} %collective-permute-done.23.refs_0_), channel_id=1, source_target_pairs={{0,8},{8,0},{16,24},{24,16},{32,40},{40,32},{48,56},{56,48},{64,72... | collective-permute-start | bytes 909320 | tf_op jit(solution)/shard_map/ppermute | solution.py:170
  25.0 29.0 %collective-permute-start.20 = (bf16[592,256]{1,0:T(8,128)(2,1)}, bf16[592,256]{1,0:T(8,128)(2,1)}, u32[]{:S(2)}, u32[]{:S(2)}) collective-permute-start(bf16[592,256]{1,0:T(8,128)(2,1)} %collective-permute-done.refs_2_), channel_id=1, source_target_pairs={{32,48},{40,56},{48,32},{56,40},{64,80},{72,88},{80,64},{88,72},{9... | collective-permute-start | bytes 909320 | tf_op jit(solution)/shard_map/ppermute | solution.py:170
  31.3 1.0 copy-start.2
  44.3 17.7 %collective-permute-start.15 = (bf16[592,256]{1,0:T(8,128)(2,1)S(1)}, bf16[592,256]{1,0:T(8,128)(2,1)S(1)}, u32[]{:S(2)}, u32[]{:S(2)}) collective-permute-start(bf16[592,256]{1,0:T(8,128)(2,1)S(1)} %collective-permute-done.6.refs_4_), channel_id=1, source_target_pairs={{160,168},{168,160},{176,184},{184,176},{192,200},{200,192},{208,2... | collective-permute-start | bytes 909320 | tf_op jit(solution)/shard_map/ppermute | solution.py:170
  46.3 22.1 %collective-permute-start.22 = (bf16[592,256]{1,0:T(8,128)(2,1)}, bf16[592,256]{1,0:T(8,128)(2,1)S(1)}, u32[]{:S(2)}, u32[]{:S(2)}) collective-permute-start(bf16[592,256]{1,0:T(8,128)(2,1)} %collective-permute-done.1.refs_2_), channel_id=1, source_target_pairs={{64,72},{72,64},{80,88},{88,80},{96,104},{104,96},{112,120},{120,1... | collective-permute-start | bytes 909320 | tf_op jit(solution)/shard_map/ppermute | solution.py:170
  48.7 17.7 %collective-permute-start.2 = (bf16[592,256]{1,0:T(8,128)(2,1)}, bf16[592,256]{1,0:T(8,128)(2,1)S(1)}, u32[]{:S(2)}, u32[]{:S(2)}) collective-permute-start(bf16[592,256]{1,0:T(8,128)(2,1)} %collective-permute-done.1.refs_2_), channel_id=1, source_target_pairs={{64,96},{72,104},{80,112},{88,120},{96,128},{104,136},{112,144},{1... | collective-permute-start | bytes 909320 | tf_op jit(solution)/shard_map/ppermute | solution.py:170
  50.6 21.6 %collective-permute-start.17 = (bf16[592,256]{1,0:T(8,128)(2,1)}, bf16[592,256]{1,0:T(8,128)(2,1)S(1)}, u32[]{:S(2)}, u32[]{:S(2)}) collective-permute-start(bf16[592,256]{1,0:T(8,128)(2,1)} %collective-permute-done.1.refs_2_), channel_id=1, source_target_pairs={{64,80},{72,88},{80,64},{88,72},{96,112},{104,120},{112,96},{120,1... | collective-permute-start | bytes 909320 | tf_op jit(solution)/shard_map/ppermute | solution.py:170
  54.1 16.3 %collective-permute-start.21 = (bf16[592,256]{1,0:T(8,128)(2,1)}, bf16[592,256]{1,0:T(8,128)(2,1)S(1)}, u32[]{:S(2)}, u32[]{:S(2)}) collective-permute-start(bf16[592,256]{1,0:T(8,128)(2,1)} %collective-permute-done.20.refs_0_), channel_id=1, source_target_pairs={{32,40},{40,32},{48,56},{56,48},{64,72},{72,64},{80,88},{88,80},{9... | collective-permute-start | bytes 909320 | tf_op jit(solution)/shard_map/ppermute | solution.py:170
  62.1 20.4 %collective-permute-start.16 = (bf16[592,256]{1,0:T(8,128)(2,1)S(1)}, bf16[592,256]{1,0:T(8,128)(2,1)S(1)}, u32[]{:S(2)}, u32[]{:S(2)}) collective-permute-start(bf16[592,256]{1,0:T(8,128)(2,1)S(1)} %collective-permute-done.9.refs_6_), channel_id=1, source_target_pairs={{192,200},{200,192},{208,216},{216,208},{224,232},{232,224},{240,2... | collective-permute-start | bytes 909320 | tf_op jit(solution)/shard_map/ppermute | solution.py:170
  66.4 21.6 %collective-permute-start.19 = (bf16[592,256]{1,0:T(8,128)(2,1)S(1)}, bf16[592,256]{1,0:T(8,128)(2,1)S(1)}, u32[]{:S(2)}, u32[]{:S(2)}) collective-permute-start(bf16[592,256]{1,0:T(8,128)(2,1)S(1)} %collective-permute-done.2.refs_2_), channel_id=1, source_target_pairs={{96,104},{104,96},{112,120},{120,112},{128,136},{136,128},{144,152... | collective-permute-start | bytes 909320 | tf_op jit(solution)/shard_map/ppermute | solution.py:170
  68.4 21.6 %collective-permute-start.3 = (bf16[592,256]{1,0:T(8,128)(2,1)S(1)}, bf16[592,256]{1,0:T(8,128)(2,1)S(1)}, u32[]{:S(2)}, u32[]{:S(2)}) collective-permute-start(bf16[592,256]{1,0:T(8,128)(2,1)S(1)} %collective-permute-done.2.refs_2_), channel_id=1, source_target_pairs={{96,128},{104,136},{112,144},{120,152},{128,160},{136,168},{144,17... | collective-permute-start | bytes 909320 | tf_op jit(solution)/shard_map/ppermute | solution.py:170
  70.3 25.6 %collective-permute-start.12 = (bf16[592,256]{1,0:T(8,128)(2,1)S(1)}, bf16[592,256]{1,0:T(8,128)(2,1)S(1)}, u32[]{:S(2)}, u32[]{:S(2)}) collective-permute-start(bf16[592,256]{1,0:T(8,128)(2,1)S(1)} %collective-permute-done.2.refs_2_), channel_id=1, source_target_pairs={{96,112},{104,120},{112,96},{120,104},{128,144},{136,152},{144,128... | collective-permute-start | bytes 909320 | tf_op jit(solution)/shard_map/ppermute | solution.py:170
  72.3 19.7 %collective-permute-start.18 = (bf16[592,256]{1,0:T(8,128)(2,1)S(1)}, bf16[592,256]{1,0:T(8,128)(2,1)S(1)}, u32[]{:S(2)}, u32[]{:S(2)}) collective-permute-start(bf16[592,256]{1,0:T(8,128)(2,1)S(1)} %collective-permute-done.17.refs_0_), channel_id=1, source_target_pairs={{64,72},{72,64},{80,88},{88,80},{96,104},{104,96},{112,120},{120,1... | collective-permute-start | bytes 909320 | tf_op jit(solution)/shard_map/ppermute | solution.py:170
  82.5 21.4 %collective-permute-start.10 = (bf16[592,256]{1,0:T(8,128)(2,1)S(1)}, bf16[592,256]{1,0:T(8,128)(2,1)S(1)}, u32[]{:S(2)}, u32[]{:S(2)}) collective-permute-start(bf16[592,256]{1,0:T(8,128)(2,1)S(1)} %collective-permute-done.9.refs_6_), channel_id=1, source_target_pairs={{192,208},{200,216},{208,192},{216,200},{224,240},{232,248},{240,2... | collective-permute-start | bytes 909320 | tf_op jit(solution)/shard_map/ppermute | solution.py:170
  88.1 18.0 %collective-permute-start.7 = (bf16[592,256]{1,0:T(8,128)(2,1)S(1)}, bf16[592,256]{1,0:T(8,128)(2,1)S(1)}, u32[]{:S(2)}, u32[]{:S(2)}) collective-permute-start(bf16[592,256]{1,0:T(8,128)(2,1)S(1)} %collective-permute-done.6.refs_4_), channel_id=1, source_target_pairs={{160,176},{168,184},{176,160},{184,168},{192,208},{200,216},{208,1... | collective-permute-start | bytes 909320 | tf_op jit(solution)/shard_map/ppermute | solution.py:170
  90.0 20.4 %collective-permute-start.14 = (bf16[592,256]{1,0:T(8,128)(2,1)S(1)}, bf16[592,256]{1,0:T(8,128)(2,1)S(1)}, u32[]{:S(2)}, u32[]{:S(2)}) collective-permute-start(bf16[592,256]{1,0:T(8,128)(2,1)S(1)} %collective-permute-done.3.refs_2_), channel_id=1, source_target_pairs={{128,136},{136,128},{144,152},{152,144},{160,168},{168,160},{176,1... | collective-permute-start | bytes 909320 | tf_op jit(solution)/shard_map/ppermute | solution.py:170
  92.0 16.3 %collective-permute-start.4 = (bf16[592,256]{1,0:T(8,128)(2,1)S(1)}, bf16[592,256]{1,0:T(8,128)(2,1)S(1)}, u32[]{:S(2)}, u32[]{:S(2)}) collective-permute-start(bf16[592,256]{1,0:T(8,128)(2,1)S(1)} %collective-permute-done.3.refs_2_), channel_id=1, source_target_pairs={{128,144},{136,152},{144,128},{152,136},{160,176},{168,184},{176,1... | collective-permute-start | bytes 909320 | tf_op jit(solution)/shard_map/ppermute | solution.py:170
  95.9 14.6 %collective-permute-start.13 = (bf16[592,256]{1,0:T(8,128)(2,1)S(1)}, bf16[592,256]{1,0:T(8,128)(2,1)S(1)}, u32[]{:S(2)}, u32[]{:S(2)}) collective-permute-start(bf16[592,256]{1,0:T(8,128)(2,1)S(1)} %collective-permute-done.12.refs_0_), channel_id=1, source_target_pairs={{96,104},{104,96},{112,120},{120,112},{128,136},{136,128},{144,152... | collective-permute-start | bytes 909320 | tf_op jit(solution)/shard_map/ppermute | solution.py:170
  103.9 20.4 %collective-permute-start.11 = (bf16[592,256]{1,0:T(8,128)(2,1)S(1)}, bf16[592,256]{1,0:T(8,128)(2,1)S(1)}, u32[]{:S(2)}, u32[]{:S(2)}) collective-permute-start(bf16[592,256]{1,0:T(8,128)(2,1)S(1)} %collective-permute-done.10.refs_4_), channel_id=1, source_target_pairs={{192,200},{200,192},{208,216},{216,208},{224,232},{232,224},{240,2... | collective-permute-start | bytes 909320 | tf_op jit(solution)/shard_map/ppermute | solution.py:170
  106.1 18.2 %collective-permute-start.8 = (bf16[592,256]{1,0:T(8,128)(2,1)S(1)}, bf16[592,256]{1,0:T(8,128)(2,1)S(1)}, u32[]{:S(2)}, u32[]{:S(2)}) collective-permute-start(bf16[592,256]{1,0:T(8,128)(2,1)S(1)} %collective-permute-done.7.refs_2_), channel_id=1, source_target_pairs={{160,168},{168,160},{176,184},{184,176},{192,200},{200,192},{208,2... | collective-permute-start | bytes 909320 | tf_op jit(solution)/shard_map/ppermute | solution.py:170
  108.3 16.1 %collective-permute-start.5 = (bf16[592,256]{1,0:T(8,128)(2,1)S(1)}, bf16[592,256]{1,0:T(8,128)(2,1)S(1)}, u32[]{:S(2)}, u32[]{:S(2)}) collective-permute-start(bf16[592,256]{1,0:T(8,128)(2,1)S(1)} %collective-permute-done.4.refs_0_), channel_id=1, source_target_pairs={{128,136},{136,128},{144,152},{152,144},{160,168},{168,160},{176,1... | collective-permute-start | bytes 909320 | tf_op jit(solution)/shard_map/ppermute | solution.py:170
  110.5 13.9 %copy-start = (bf16[1,8,512,128]{3,2,1,0:T(8,128)(2,1)S(1)}, bf16[1,8,512,128]{3,2,1,0:T(8,128)(2,1)}, u32[]{:S(2)}) copy-start(bf16[1,8,512,128]{3,2,1,0:T(8,128)(2,1)} %param.9) | copy-start | bytes 3145732
  132.9 17.8 %collective-permute-start.27 = (bf16[1,256,1024]{2,1,0:T(8,128)(2,1)S(1)}, bf16[1,256,1024]{2,1,0:T(8,128)(2,1)S(1)}, u32[]{:S(2)}, u32[]{:S(2)}) collective-permute-start(bf16[1,256,1024]{2,1,0:T(8,128)(2,1)S(1)} %bitcast.13), channel_id=1, source_target_pairs={{0,1},{1,2},{2,3},{3,4},{4,5},{5,6},{6,7},{7,0},{8,9},{9,10},{10,1... | collective-permute-start | bytes 1572872 | tf_op jit(solution)/shard_map/ppermute | solution.py:211

commit v2 on v1

v2 whole, which is shorter than its diff:
```python
import functools
import jax
import jax.numpy as jnp
from jax import lax
from jax.experimental import pallas as pl
from jax.experimental.pallas import tpu as pltpu
from jax.sharding import PartitionSpec as P

very_low = -1e30
log2_e = 1.4426950408889634
id_rows = 16
documents = 8


def dot(a, b, of_a, of_b):
    return lax.dot_general(a, b, (((of_a,), (of_b,)), ((), ())), preferred_element_type=jnp.float32)


def origin_of(me, place, e):
    step, across, swapped = place
    holder = me ^ (2 * across + swapped)
    if step == 0:
        return holder ^ e
    back = jnp.where((holder & 1) == 0, step, 7 - step)
    return (holder ^ e) - 4 * back


def attend(places, first, final, factor_scale, info, ids_v, queries, *refs):
    pieces, refs = refs[: len(places)], refs[len(places) :]
    if final:
        up, refs = refs[0], refs[1:]
    if not first:
        refs = refs[3:]
    (peak, total, accum), refs = refs[:3], refs[3:]
    if final:
        out, refs = refs[0], refs[1:]
    flipped, values, bias, score_buf, weight_buf, factor_buf = refs
    heads, latent, tokens = accum.shape
    width = queries.shape[0] // heads
    me = info[0, 0]
    first_id = info[0, 1]
    blocks = []
    for piece, place in zip(pieces, places):
        for e in range(piece.shape[0]):
            blocks.append((piece.at[e], place, e))
    if first:
        peak[...] = jnp.full(peak.shape, very_low, jnp.float32)
        total[...] = jnp.zeros(total.shape, jnp.float32)
        accum[...] = jnp.zeros(accum.shape, jnp.float32)
    query_ids = ids_v[...]
    key_at = lax.broadcasted_iota(jnp.int32, (tokens, tokens), 0)
    first_float = first_id.astype(jnp.float32)
    key_ids = [b[width : width + id_rows, :].astype(jnp.float32)[0:1, :] for b, _, _ in blocks]
    counts = [jnp.sum(jnp.where(k < first_float, 1.0, 0.0), axis=1, keepdims=True) for k in key_ids]
    befores = [c[0, 0].astype(jnp.int32) for c in counts]
    live_count = jnp.int32(0)
    for (block, place, e), ids_here, before in zip(blocks, key_ids, befores):
        own = place == (0, 0, 0) and e == 0
        origin = origin_of(me, place, e)
        if own:
            live = jnp.bool_(True)
        else:
            hit = info[0, 2 + jnp.maximum(origin, 0)]
            live = (origin >= 0) & (origin < me) & (hit == 1) & (before < tokens)

        def pack(block=block, ids_here=ids_here, before=before, slot=live_count, own=own):
            flipped[slot] = block[0:width, :].T
            values[slot] = block[0:latent, :]
            if own:
                start = jnp.zeros(query_ids.shape, jnp.int32)
                for d in range(documents):
                    below = jnp.sum(jnp.where(ids_here < float(d), 1.0, 0.0), axis=1, keepdims=True)
                    start = jnp.where(query_ids == d, below.astype(jnp.int32), start)
                query_at = lax.broadcasted_iota(jnp.int32, (tokens, tokens), 1)
                allowed = (key_at >= start) & (key_at <= query_at)
            else:
                allowed = (key_at >= before) & (query_ids == first_id)
            bias[slot] = jnp.where(allowed, 0.0, very_low)

        if own:
            pack()
        else:
            pl.when(live)(pack)
        live_count = live_count + live.astype(jnp.int32)

    def score(slot, head, half):
        rows = queries[head * width : (head + 1) * width, :]
        score_buf[half] = dot(flipped[slot], rows, 1, 0) + bias[slot]

    def weigh(head, half):
        scores = score_buf[half]
        old = peak[head : head + 1, :]
        new = jnp.maximum(old, jnp.max(scores, axis=0, keepdims=True))
        factor = jnp.exp2((old - new) * factor_scale)
        weights = jnp.exp2((scores - new) * factor_scale)
        total[head : head + 1, :] = total[head : head + 1, :] * factor + jnp.sum(weights, axis=0, keepdims=True)
        peak[head : head + 1, :] = new
        factor_buf[half] = jnp.broadcast_to(factor, factor_buf.shape[1:])
        weight_buf[half] = weights.astype(jnp.bfloat16)

    def mix(slot, head, half):
        accum[head] = accum[head] * factor_buf[half][0:1, :] + dot(values[slot], weight_buf[half], 1, 0)

    @pl.when(live_count > 0)
    def _():
        weight_buf[1] = jnp.zeros(weight_buf.shape[1:], weight_buf.dtype)
        factor_buf[1] = jnp.ones(factor_buf.shape[1:], factor_buf.dtype)
        score(0, 0, 0)

        def over_live(slot, carry):
            after, prior = jnp.minimum(slot + 1, live_count - 1), jnp.maximum(slot - 1, 0)
            for head in range(heads):
                half = head % 2
                score(slot if head < heads - 1 else after, (head + 1) % heads, 1 - half)
                weigh(head, half)
                mix(slot if head > 0 else prior, (head - 1) % heads, 1 - half)
            return carry

        lax.fori_loop(0, live_count, over_live, 0)
        mix(live_count - 1, heads - 1, (heads - 1) % 2)

    if final:
        value_width = up.shape[2]
        for head in range(heads):
            mixed = (accum[head] / total[head : head + 1, :]).astype(jnp.bfloat16)
            part = dot(up[head], mixed, 0, 0)
            out[:, head * value_width : (head + 1) * value_width] = part.T.astype(jnp.bfloat16)


def stage(places, pieces, info, ids, queries, state, up, sizes):
    heads, latent, tokens, width, value_width = sizes
    first, final = state is None, up is not None
    count = sum(p.shape[0] for p in pieces)
    scalars, vectors = pl.BlockSpec(memory_space=pltpu.SMEM), pl.BlockSpec(memory_space=pltpu.VMEM)
    shapes = [((heads, tokens), jnp.float32), ((heads, tokens), jnp.float32), ((heads, latent, tokens), jnp.float32)]
    operands = [info, ids, queries, *pieces]
    specs = [scalars, vectors, vectors] + [vectors] * len(pieces)
    aliases = {}
    out_shape = [pltpu.VMEM(shape, dtype) for shape, dtype in shapes]
    if final:
        operands.append(up)
        specs.append(vectors)
        out_shape.append(jax.ShapeDtypeStruct((tokens, heads * value_width), jnp.bfloat16))
    if not first:
        aliases = {len(operands) + i: i for i in range(3)}
        operands += [pltpu.with_memory_space_constraint(x, pltpu.VMEM) for x in state]
        specs += [vectors] * 3
    scratch = [
        pltpu.VMEM((count, tokens, width), jnp.bfloat16),
        pltpu.VMEM((count, latent, tokens), jnp.bfloat16),
        pltpu.VMEM((count, tokens, tokens), jnp.float32),
        pltpu.VMEM((2, tokens, tokens), jnp.float32),
        pltpu.VMEM((2, tokens, tokens), jnp.bfloat16),
        pltpu.VMEM((2, 8, tokens), jnp.float32),
    ]
    scale = (value_width + width - latent) ** -0.5 * log2_e
    work = 2 * count * heads * tokens * tokens * (width + latent)
    result = pl.pallas_call(
        functools.partial(attend, tuple(places), first, final, scale),
        out_shape=out_shape,
        in_specs=specs,
        out_specs=[vectors] * len(out_shape),
        scratch_shapes=scratch,
        input_output_aliases=aliases,
        cost_estimate=pl.CostEstimate(
            flops=work, bytes_accessed=count * 2 * width * tokens, transcendentals=count * heads * tokens * tokens
        ),
        compiler_params=pltpu.CompilerParams(vmem_limit_bytes=24 * 2**20),
        name="attend",
    )(*operands)
    return result[3] if final else list(result)


def tie(*arrays):
    return list(lax.optimization_barrier(tuple(arrays)))


def shards(queries, latent_cache, doc_ids, block_table, w_uv):
    tokens, heads, latent, value_width = queries.shape[1], w_uv.shape[1], w_uv.shape[2], w_uv.shape[3]
    width = latent_cache.shape[1]
    sizes = (heads, latent, tokens, width, value_width)
    devices = lax.axis_size("ctx")
    planes = devices // 4
    me = lax.axis_index("ctx")

    def across(x, step=0):
        return lax.ppermute(x, "ctx", [(i, i ^ 2) for i in range(devices) if i // 4 >= least(step, i % 2)])

    def core(x, step=0):
        return lax.ppermute(x, "ctx", [(i, i ^ 1) for i in range(devices) if i // 4 >= least(step, i % 2)])

    def least(step, odd):
        return 0 if step == 0 else step if odd == 0 else planes - 1 - step

    def along(x, step):
        pairs = []
        for i in range(devices):
            plane = i // 4
            if i % 2 == 0:
                if step - 1 <= plane < planes - 1:
                    pairs.append((i, i + 4))
            else:
                source = (plane + step) % planes if step > 1 else plane
                if source < planes // 2:
                    pairs.append((i, (i - (8 if step == 1 else 4)) % devices))
        return lax.ppermute(x, "ctx", pairs)

    ids = jnp.broadcast_to(doc_ids.astype(jnp.bfloat16), (id_rows, tokens))
    own = jnp.concatenate([latent_cache[0], ids], axis=0)[None]
    c0, x0 = core(own), across(own)
    row = lax.dynamic_slice_in_dim(block_table, me, 1, 0)
    info = jnp.concatenate([jnp.full((1, 1), me, jnp.int32), doc_ids[:, :1], row], axis=1)
    queries_t = pltpu.with_memory_space_constraint(queries[0].T, pltpu.VMEM)

    def run(places, pieces, state, up=None):
        return stage(places, pieces, info, doc_ids, queries_t, state, up, sizes)

    pair = jnp.concatenate([own, c0], axis=0)
    z1 = along(pair, 1)
    cx0 = core(x0)
    state = run([(0, 0, 0)], [pair], None)
    state = run([(0, 1, 0), (0, 1, 1)], [x0, cx0], state)
    z2, x1 = along(z1, 2), across(z1, 1)
    *state, z1 = tie(*state, z1)
    state = run([(1, 0, 0)], [z1], state)
    *state, z1, z2 = tie(*state, z1, z2)
    cz1 = core(z1, 1)
    z3 = along(z2, 3)
    state = run([(1, 0, 1)], [cz1], state)
    *state, z2, x1 = tie(*state, z2, x1)
    x2 = across(z2, 2)
    state = run([(1, 1, 0)], [x1], state)
    *state, x1, z3 = tie(*state, x1, z3)
    cx1 = core(x1, 1)
    state = run([(2, 0, 0)], [z2], state)
    *state, z3, cx1 = tie(*state, z3, cx1)
    x3 = across(z3, 3)
    state = run([(1, 1, 1)], [cx1], state)
    *state, z2 = tie(*state, z2)
    cz2 = core(z2, 2)
    state = run([(3, 0, 0)], [z3], state)
    *state, z3, cz2 = tie(*state, z3, cz2)
    cz3 = core(z3, 3)
    state = run([(2, 0, 1)], [cz2], state)
    *state, x2, cz3 = tie(*state, x2, cz3)
    cx2 = core(x2, 2)
    state = run([(2, 1, 0), (3, 0, 1)], [x2, cz3], state)
    *state, x3, cx2 = tie(*state, x3, cx2)
    cx3 = core(x3, 3)
    state = run([(2, 1, 1), (3, 1, 0)], [cx2, x3], state)
    heads_out = run([(3, 1, 1)], [cx3], state, w_uv[0])
    sections = lax.axis_size("section")
    return lax.ppermute(heads_out[None], "section", [(i, (i + 1) % sections) for i in range(sections)])


def solution(mesh):
    placed = (
        P("section", "ctx", None),
        P("section", None, "ctx"),
        P("section", "ctx"),
        P(),
        P("section", None, None, None),
    )
    return jax.shard_map(
        shards, mesh=mesh, in_specs=placed, out_specs=P("section", "ctx", None), check_vma=False
    )
```

time: 154 us -> 140 us (0.909)
  the two profiles are of different devices: /device:TPU:194 before, /device:TPU:248 now
where the time goes in v2:
time: 140 us; the launch traced here: 141 us
  Pallas kernels  47.1 us (34%)
  waiting for transfers between devices  43.8 us (31%)
  starting transfers between devices  41 us (29%)
  local copies, waits for them, and re-layouts  4.88 us (3%)
  other arithmetic  4.19 us (3%)
    pallas_call x12, Pallas kernels, stage(): pl.pallas_call(functools.partial(attend, tuple(places), first, final, sca...  47.1 us
    ppermute x4, waiting for transfers between devices, across(): lax.ppermute(x, 'ctx', [(i, i ^ 2) for i in range(devices) if i // 4 >= l...  25.4 us
    ppermute x8, starting transfers between devices, core(): lax.ppermute(x, 'ctx', [(i, i ^ 1) for i in range(devices) if i // 4 >= l...  23 us
    ppermute x1, waiting for transfers between devices, shards(): lax.ppermute(heads_out[None], 'section', [(i, (i + 1) % sections) for i i...  14.8 us
    ppermute x4, starting transfers between devices, across(): lax.ppermute(x, 'ctx', [(i, i ^ 2) for i in range(devices) if i // 4 >= l...  14 us
    ppermute x3, starting transfers between devices, along(): return lax.ppermute(x, 'ctx', pairs)  3.86 us
    unnamed x8, local copies, waits for them, and re-layouts  3.63 us
  transfers between devices with their start and end apart: 16, of which 8 were waited for; matrix products, arithmetic and copies ran while one was open for 3% of the time, Pallas kernels for 27%

profile of v2, /device:TPU:248, one launch (start us, length us, event | category | flops | bytes accessed | tf_op | source)
XLA Modules:
  0.0 141.3 jit_solution(3556855758129804604)
XLA Ops:
  0.0 0.0 copy-start
  0.0 0.0 copy-start.2
  0.0 0.8 convert_reduce_fusion
  0.8 1.7 %maximum_bitcast_fusion = bf16[1,592,256]{2,1,0:T(8,128)(2,1)} fusion(bf16[16,256]{1,0:T(8,128)(2,1)S(1)} %broadcast_in_dim.18, bf16[576,256]{1,0:T(8,128)(2,1)} %bitcast.23), kind=kLoop, calls=%fused_computation.1 | loop fusion | flops 606208 | bytes 606208 | tf_op jit(solution)/shard_map/broadcast_in_dim | solution.py:209
  2.5 0.0 collective-permute-start.2
  2.5 1.8 %collective-permute-done.2 = bf16[1,592,256]{2,1,0:T(8,128)(2,1)S(1)} collective-permute-done((bf16[1,592,256]{2,1,0:T(8,128)(2,1)}, bf16[1,592,256]{2,1,0:T(8,128)(2,1)S(1)}, u32[]{:S(2)}, u32[]{:S(2)}) %collective-permute-start.2) | collective-permute-done | bytes 303136 | tf_op jit(solution)/shard_map/ppermute | solution.py:190
  4.3 1.0 pad_maximum_fusion.refs_0_
  5.3 1.3 collective-permute-start.3
  6.6 1.6 %collective-permute-start = (bf16[1,592,256]{2,1,0:T(8,128)(2,1)}, bf16[1,592,256]{2,1,0:T(8,128)(2,1)S(1)}, u32[]{:S(2)}, u32[]{:S(2)}) collective-permute-start(bf16[1,592,256]{2,1,0:T(8,128)(2,1)} %maximum_bitcast_fusion), channel_id=1, source_target_pairs={{0,16},{8,24},{16,0},{24,8},{32,48},{40,56},{48,32},{56,40},{64,80... | collective-permute-start | bytes 909320 | tf_op jit(solution)/shard_map/ppermute | solution.py:187
  8.2 1.2 slice.3
  9.4 2.8 %copy.39 = bf16[1,256,4608]{1,2,0:T(8,128)(2,1)S(1)} copy(bf16[1,256,4608]{2,1,0:T(8,128)(2,1)} %param.5) | data formatting | bytes 4718592 | tf_op args[0]
  12.2 0.0 copy-done
  12.3 3.9 %collective-permute-done.refs_0_ = bf16[1,592,256]{2,1,0:T(8,128)(2,1)S(1)} collective-permute-done((bf16[1,592,256]{2,1,0:T(8,128)(2,1)}, bf16[1,592,256]{2,1,0:T(8,128)(2,1)S(1)}, u32[]{:S(2)}, u32[]{:S(2)}) %collective-permute-start) | collective-permute-done | bytes 303136 | tf_op jit(solution)/shard_map/ppermute | solution.py:187
  16.1 0.0 collective-permute-start.1
  16.1 0.7 pad_add_fusion.info
  16.8 0.5 collective-permute-done.3.refs_0_
  17.4 1.3 collective-permute-start.4
  18.7 0.0 copy-done.2
  18.7 3.2 %attend.12 = (f32[8,256]{1,0:T(8,128)S(1)}, f32[8,256]{1,0:T(8,128)S(1)}, f32[8,512,256]{2,1,0:T(8,128)S(1)}) custom-call(s32[1,34]{1,0:T(1,128)S(1)} %pad_add_fusion.info, s32[1,256]{1,0:T(1,128)S(1)} %copy-done.2, bf16[4608,256]{1,0:T(8,128)(2,1)S(1)} %bitcast.9, bf16[2,592,256]{2,1,0:T(8,128)(2,1)S(1)} %pad_maximum_fusion.refs_0_), custom_call_target="tpu_custom_call" | custom-call | flops 2281701376 | bytes 589824 | tf_op jit(solution)/shard_map/attend/pallas_call | solution.py:158
  21.9 0.0 collective-permute-done.1.refs_1_
  21.9 0.7 attend.13
  22.6 5.6 %attend.14 = (f32[8,256]{1,0:T(8,128)S(1)}, f32[8,256]{1,0:T(8,128)S(1)}, f32[8,512,256]{2,1,0:T(8,128)S(1)}) custom-call(s32[1,34]{1,0:T(1,128)S(1)} %pad_add_fusion.info, s32[1,256]{1,0:T(1,128)S(1)} %copy-done.2, bf16[4608,256]{1,0:T(8,128)(2,1)S(1)} %bitcast.11, ...), custom_call_target="tpu_custom_call", output_to_operand_aliasing={{0}: (4, {}), {1}: (5, {}), {2}: (6, {})} | custom-call | flops 2281701376 | bytes 589824 | tf_op jit(solution)/shard_map/attend/pallas_call | solution.py:158
  28.2 1.3 collective-permute-done.4.refs_0_
  29.5 8.2 %collective-permute-start.5 = (bf16[2,592,256]{2,1,0:T(8,128)(2,1)}, bf16[2,592,256]{2,1,0:T(8,128)(2,1)S(1)}, u32[]{:S(2)}, u32[]{:S(2)}) collective-permute-start(bf16[2,592,256]{2,1,0:T(8,128)(2,1)} %collective-permute-done.3.refs_0_), channel_id=1, source_target_pairs={{32,40},{48,56},{64,72},{80,88},{96,104},{112,120},{128,136},{144,... | collective-permute-start | bytes 1818632 | tf_op jit(solution)/shard_map/ppermute | solution.py:190
  37.8 6.6 %collective-permute-start.6 = (bf16[2,592,256]{2,1,0:T(8,128)(2,1)}, bf16[2,592,256]{2,1,0:T(8,128)(2,1)S(1)}, u32[]{:S(2)}, u32[]{:S(2)}) collective-permute-start(bf16[2,592,256]{2,1,0:T(8,128)(2,1)} %collective-permute-done.3.refs_0_), channel_id=1, source_target_pairs={{32,48},{48,32},{64,80},{80,64},{96,112},{112,96},{128,144},{144,1... | collective-permute-start | bytes 1818632 | tf_op jit(solution)/shard_map/ppermute | solution.py:187
  44.4 1.3 collective-permute-start.7
  45.7 0.0 collective-permute-done.5.refs_0_
  45.7 0.7 attend.15
  46.4 12.0 %collective-permute-done.6.refs_0_ = bf16[2,592,256]{2,1,0:T(8,128)(2,1)S(1)} collective-permute-done((bf16[2,592,256]{2,1,0:T(8,128)(2,1)}, bf16[2,592,256]{2,1,0:T(8,128)(2,1)S(1)}, u32[]{:S(2)}, u32[]{:S(2)}) %collective-permute-start.6) | collective-permute-done | bytes 606240 | tf_op jit(solution)/shard_map/ppermute | solution.py:187
  58.4 5.2 %attend.16 = (f32[8,256]{1,0:T(8,128)S(1)}, f32[8,256]{1,0:T(8,128)S(1)}, f32[8,512,256]{2,1,0:T(8,128)S(1)}) custom-call(s32[1,34]{1,0:T(1,128)S(1)} %pad_add_fusion.info, s32[1,256]{1,0:T(1,128)S(1)} %copy-done.2, bf16[4608,256]{1,0:T(8,128)(2,1)S(1)} %bitcast.13, ...), custom_call_target="tpu_custom_call", output_to_operand_aliasing={{0}: (4, {}), {1}: (5, {}), {2}: (6, {})} | custom-call | flops 2281701376 | bytes 589824 | tf_op jit(solution)/shard_map/attend/pallas_call | solution.py:158
  63.6 0.0 collective-permute-done.7.refs_0_
  63.7 1.9 %collective-permute-start.8 = (bf16[2,592,256]{2,1,0:T(8,128)(2,1)S(1)}, bf16[2,592,256]{2,1,0:T(8,128)(2,1)S(1)}, u32[]{:S(2)}, u32[]{:S(2)}) collective-permute-start(bf16[2,592,256]{2,1,0:T(8,128)(2,1)S(1)} %collective-permute-done.6.refs_0_), channel_id=1, source_target_pairs={{32,40},{48,56},{64,72},{80,88},{96,104},{112,120},{128,136},{144,... | collective-permute-start | bytes 1818632 | tf_op jit(solution)/shard_map/ppermute | solution.py:190
  65.6 5.0 %attend.17 = (f32[8,256]{1,0:T(8,128)S(1)}, f32[8,256]{1,0:T(8,128)S(1)}, f32[8,512,256]{2,1,0:T(8,128)S(1)}) custom-call(s32[1,34]{1,0:T(1,128)S(1)} %pad_add_fusion.info, s32[1,256]{1,0:T(1,128)S(1)} %copy-done.2, bf16[4608,256]{1,0:T(8,128)(2,1)S(1)} %bitcast.14, ...), custom_call_target="tpu_custom_call", output_to_operand_aliasing={{0}: (4, {}), {1}: (5, {}), {2}: (6, {})} | custom-call | flops 2281701376 | bytes 589824 | tf_op jit(solution)/shard_map/attend/pallas_call | solution.py:158
  70.6 0.0 collective-permute-done.8.refs_0_
  70.6 3.1 %attend.18 = (f32[8,256]{1,0:T(8,128)S(1)}, f32[8,256]{1,0:T(8,128)S(1)}, f32[8,512,256]{2,1,0:T(8,128)S(1)}) custom-call(s32[1,34]{1,0:T(1,128)S(1)} %pad_add_fusion.info, s32[1,256]{1,0:T(1,128)S(1)} %copy-done.2, bf16[4608,256]{1,0:T(8,128)(2,1)S(1)} %bitcast.15, ...), custom_call_target="tpu_custom_call", output_to_operand_aliasing={{0}: (4, {}), {1}: (5, {}), {2}: (6, {})} | custom-call | flops 2281701376 | bytes 589824 | tf_op jit(solution)/shard_map/attend/pallas_call | solution.py:158
  73.7 4.4 %collective-permute-start.9 = (bf16[2,592,256]{2,1,0:T(8,128)(2,1)S(1)}, bf16[2,592,256]{2,1,0:T(8,128)(2,1)S(1)}, u32[]{:S(2)}, u32[]{:S(2)}) collective-permute-start(bf16[2,592,256]{2,1,0:T(8,128)(2,1)S(1)} %collective-permute-done.4.refs_0_), channel_id=1, source_target_pairs={{64,72},{80,88},{96,104},{112,120},{128,136},{144,152},{160,168},{... | collective-permute-start | bytes 1818632 | tf_op jit(solution)/shard_map/ppermute | solution.py:190
  78.1 1.9 %collective-permute-start.10 = (bf16[2,592,256]{2,1,0:T(8,128)(2,1)S(1)}, bf16[2,592,256]{2,1,0:T(8,128)(2,1)S(1)}, u32[]{:S(2)}, u32[]{:S(2)}) collective-permute-start(bf16[2,592,256]{2,1,0:T(8,128)(2,1)S(1)} %collective-permute-done.4.refs_0_), channel_id=1, source_target_pairs={{64,80},{80,64},{96,112},{112,96},{128,144},{144,128},{160,176},{1... | collective-permute-start | bytes 1818632 | tf_op jit(solution)/shard_map/ppermute | solution.py:187
  80.0 0.7 attend.19
  80.7 0.0 collective-permute-done.9.refs_0_
  80.7 4.3 %collective-permute-start.11 = (bf16[2,592,256]{2,1,0:T(8,128)(2,1)S(1)}, bf16[2,592,256]{2,1,0:T(8,128)(2,1)S(1)}, u32[]{:S(2)}, u32[]{:S(2)}) collective-permute-start(bf16[2,592,256]{2,1,0:T(8,128)(2,1)S(1)} %collective-permute-done.7.refs_0_), channel_id=1, source_target_pairs={{96,104},{112,120},{128,136},{136,128},{144,152},{152,144},{160,16... | collective-permute-start | bytes 1818632 | tf_op jit(solution)/shard_map/ppermute | solution.py:190
  85.1 3.9 %collective-permute-start.12 = (bf16[2,592,256]{2,1,0:T(8,128)(2,1)S(1)}, bf16[2,592,256]{2,1,0:T(8,128)(2,1)S(1)}, u32[]{:S(2)}, u32[]{:S(2)}) collective-permute-start(bf16[2,592,256]{2,1,0:T(8,128)(2,1)S(1)} %collective-permute-done.7.refs_0_), channel_id=1, source_target_pairs={{96,112},{112,96},{128,144},{136,152},{144,128},{152,136},{160,176... | collective-permute-start | bytes 1818632 | tf_op jit(solution)/shard_map/ppermute | solution.py:187
  89.0 3.1 %attend.20 = (f32[8,256]{1,0:T(8,128)S(1)}, f32[8,256]{1,0:T(8,128)S(1)}, f32[8,512,256]{2,1,0:T(8,128)S(1)}) custom-call(s32[1,34]{1,0:T(1,128)S(1)} %pad_add_fusion.info, s32[1,256]{1,0:T(1,128)S(1)} %copy-done.2, bf16[4608,256]{1,0:T(8,128)(2,1)S(1)} %bitcast.17, ...), custom_call_target="tpu_custom_call", output_to_operand_aliasing={{0}: (4, {}), {1}: (5, {}), {2}: (6, {})} | custom-call | flops 2281701376 | bytes 589824 | tf_op jit(solution)/shard_map/attend/pallas_call | solution.py:158
  92.1 4.4 %collective-permute-done.10.refs_0_ = bf16[2,592,256]{2,1,0:T(8,128)(2,1)S(1)} collective-permute-done((bf16[2,592,256]{2,1,0:T(8,128)(2,1)S(1)}, bf16[2,592,256]{2,1,0:T(8,128)(2,1)S(1)}, u32[]{:S(2)}, u32[]{:S(2)}) %collective-permute-start.10) | collective-permute-done | bytes 606240 | tf_op jit(solution)/shard_map/ppermute | solution.py:187
  96.6 0.0 collective-permute-done.11.refs_1_
  96.6 1.9 %collective-permute-start.13 = (bf16[2,592,256]{2,1,0:T(8,128)(2,1)S(1)}, bf16[2,592,256]{2,1,0:T(8,128)(2,1)S(1)}, u32[]{:S(2)}, u32[]{:S(2)}) collective-permute-start(bf16[2,592,256]{2,1,0:T(8,128)(2,1)S(1)} %collective-permute-done.10.refs_0_), channel_id=1, source_target_pairs={{64,72},{80,88},{96,104},{112,120},{128,136},{144,152},{160,168},{... | collective-permute-start | bytes 1818632 | tf_op jit(solution)/shard_map/ppermute | solution.py:190
  98.5 5.1 %attend.21 = (f32[8,256]{1,0:T(8,128)S(1)}, f32[8,256]{1,0:T(8,128)S(1)}, f32[8,512,256]{2,1,0:T(8,128)S(1)}) custom-call(s32[1,34]{1,0:T(1,128)S(1)} %pad_add_fusion.info, s32[1,256]{1,0:T(1,128)S(1)} %copy-done.2, bf16[4608,256]{1,0:T(8,128)(2,1)S(1)} %bitcast.18, ...), custom_call_target="tpu_custom_call", output_to_operand_aliasing={{0}: (5, {}), {1}: (6, {}), {2}: (7, {})} | custom-call | flops 4563402752 | bytes 1179648 | tf_op jit(solution)/shard_map/attend/pallas_call | solution.py:158
  103.5 5.1 %collective-permute-done.12.refs_1_ = bf16[2,592,256]{2,1,0:T(8,128)(2,1)S(1)} collective-permute-done((bf16[2,592,256]{2,1,0:T(8,128)(2,1)S(1)}, bf16[2,592,256]{2,1,0:T(8,128)(2,1)S(1)}, u32[]{:S(2)}, u32[]{:S(2)}) %collective-permute-start.12) | collective-permute-done | bytes 606240 | tf_op jit(solution)/shard_map/ppermute | solution.py:187
  108.6 0.0 collective-permute-done.13.refs_0_
  108.6 0.0 copy-start.1
  108.6 2.3 %collective-permute-start.14 = (bf16[2,592,256]{2,1,0:T(8,128)(2,1)S(1)}, bf16[2,592,256]{2,1,0:T(8,128)(2,1)S(1)}, u32[]{:S(2)}, u32[]{:S(2)}) collective-permute-start(bf16[2,592,256]{2,1,0:T(8,128)(2,1)S(1)} %collective-permute-done.12.refs_1_), channel_id=1, source_target_pairs={{96,104},{112,120},{128,136},{136,128},{144,152},{152,144},{160,16... | collective-permute-start | bytes 1818632 | tf_op jit(solution)/shard_map/ppermute | solution.py:190
  110.9 8.9 %attend.22 = (f32[8,256]{1,0:T(8,128)S(1)}, f32[8,256]{1,0:T(8,128)S(1)}, f32[8,512,256]{2,1,0:T(8,128)S(1)}) custom-call(s32[1,34]{1,0:T(1,128)S(1)} %pad_add_fusion.info, s32[1,256]{1,0:T(1,128)S(1)} %copy-done.2, bf16[4608,256]{1,0:T(8,128)(2,1)S(1)} %bitcast.19, ...), custom_call_target="tpu_custom_call", output_to_operand_aliasing={{0}: (5, {}), {1}: (6, {}), {2}: (7, {})} | custom-call | flops 4563402752 | bytes 1179648 | tf_op jit(solution)/shard_map/attend/pallas_call | solution.py:158
  119.8 0.0 collective-permute-done.14.refs_0_
  119.8 0.0 copy-done.1
  119.8 5.8 %attend.23 = (f32[8,256]{1,0:T(8,128)S(1)}, f32[8,256]{1,0:T(8,128)S(1)}, f32[8,512,256]{2,1,0:T(8,128)S(1)}, bf16[256,1024]{1,0:T(8,128)(2,1)S(1)}) custom-call(s32[1,34]{1,0:T(1,128)S(1)} %pad_add_fusion.info, s32[1,256]{1,0:T(1,128)S(1)} %copy-done.2, bf16[4608,256]{1,0:T(8,128)(2,1)S(1)} %bitcast.20, ...), custom_call_target="tpu_custom_call", output_to_operand_aliasing={{0}: (5, {}), {1}: (6, {}), {2}: (7, {})} | custom-call | flops 2281701376 | bytes 589824 | tf_op jit(solution)/shard_map/attend/pallas_call | solution.py:158
  125.7 0.1 collective-permute-start.15
  125.7 14.8 %collective-permute-done.15 = bf16[1,256,1024]{2,1,0:T(8,128)(2,1)S(1)} collective-permute-done((bf16[1,256,1024]{2,1,0:T(8,128)(2,1)S(1)}, bf16[1,256,1024]{2,1,0:T(8,128)(2,1)S(1)}, u32[]{:S(2)}, u32[]{:S(2)}) %collective-permute-start.15) | collective-permute-done | bytes 524320 | tf_op jit(solution)/shard_map/ppermute | solution.py:253
  140.6 0.8 copy.74
  (2 shorter events, 0.0 us)
Async XLA Ops:
  0.0 12.3 %copy-start = (s32[32,32]{1,0:T(8,128)S(1)}, s32[32,32]{1,0:T(8,128)}, u32[]{:S(2)}) copy-start(s32[32,32]{1,0:T(8,128)} %param.8) | copy-start | bytes 12292
  0.0 18.7 %copy-start.2 = (s32[1,256]{1,0:T(1,128)S(1)}, s32[1,256]{1,0:T(1,128)}, u32[]{:S(2)}) copy-start(s32[1,256]{1,0:T(1,128)} %ids_v.23) | copy-start | bytes 3076
  2.5 1.8 %collective-permute-start.2 = (bf16[1,592,256]{2,1,0:T(8,128)(2,1)}, bf16[1,592,256]{2,1,0:T(8,128)(2,1)S(1)}, u32[]{:S(2)}, u32[]{:S(2)}) collective-permute-start(bf16[1,592,256]{2,1,0:T(8,128)(2,1)} %maximum_bitcast_fusion), channel_id=1, source_target_pairs={{0,8},{8,0},{16,24},{24,16},{32,40},{40,32},{48,56},{56,48},{64,72... | collective-permute-start | bytes 909320 | tf_op jit(solution)/shard_map/ppermute | solution.py:190
  5.3 12.1 %collective-permute-start.3 = (bf16[2,592,256]{2,1,0:T(8,128)(2,1)S(1)}, bf16[2,592,256]{2,1,0:T(8,128)(2,1)}, u32[]{:S(2)}, u32[]{:S(2)}) collective-permute-start(bf16[2,592,256]{2,1,0:T(8,128)(2,1)S(1)} %pad_maximum_fusion.refs_0_), channel_id=1, source_target_pairs={{0,32},{8,200},{16,48},{24,216},{32,64},{40,232},{48,80},{56,248},... | collective-permute-start | bytes 1818632 | tf_op jit(solution)/shard_map/ppermute | solution.py:206
  6.6 9.5 %collective-permute-start = (bf16[1,592,256]{2,1,0:T(8,128)(2,1)}, bf16[1,592,256]{2,1,0:T(8,128)(2,1)S(1)}, u32[]{:S(2)}, u32[]{:S(2)}) collective-permute-start(bf16[1,592,256]{2,1,0:T(8,128)(2,1)} %maximum_bitcast_fusion), channel_id=1, source_target_pairs={{0,16},{8,24},{16,0},{24,8},{32,48},{40,56},{48,32},{56,40},{64,80... | collective-permute-start | bytes 909320 | tf_op jit(solution)/shard_map/ppermute | solution.py:187
  16.1 5.8 %collective-permute-start.1 = (bf16[1,592,256]{2,1,0:T(8,128)(2,1)S(1)}, bf16[1,592,256]{2,1,0:T(8,128)(2,1)S(1)}, u32[]{:S(2)}, u32[]{:S(2)}) collective-permute-start(bf16[1,592,256]{2,1,0:T(8,128)(2,1)S(1)} %collective-permute-done.refs_0_), channel_id=1, source_target_pairs={{0,8},{8,0},{16,24},{24,16},{32,40},{40,32},{48,56},{56,48},{64,72... | collective-permute-start | bytes 909320 | tf_op jit(solution)/shard_map/ppermute | solution.py:190
  17.4 12.2 %collective-permute-start.4 = (bf16[2,592,256]{2,1,0:T(8,128)(2,1)}, bf16[2,592,256]{2,1,0:T(8,128)(2,1)S(1)}, u32[]{:S(2)}, u32[]{:S(2)}) collective-permute-start(bf16[2,592,256]{2,1,0:T(8,128)(2,1)} %collective-permute-done.3.refs_0_), channel_id=1, source_target_pairs={{8,232},{24,248},{32,64},{40,8},{48,80},{56,24},{64,96},{80,112},{... | collective-permute-start | bytes 1818632 | tf_op jit(solution)/shard_map/ppermute | solution.py:206
  29.5 16.2 %collective-permute-start.5 = (bf16[2,592,256]{2,1,0:T(8,128)(2,1)}, bf16[2,592,256]{2,1,0:T(8,128)(2,1)S(1)}, u32[]{:S(2)}, u32[]{:S(2)}) collective-permute-start(bf16[2,592,256]{2,1,0:T(8,128)(2,1)} %collective-permute-done.3.refs_0_), channel_id=1, source_target_pairs={{32,40},{48,56},{64,72},{80,88},{96,104},{112,120},{128,136},{144,... | collective-permute-start | bytes 1818632 | tf_op jit(solution)/shard_map/ppermute | solution.py:190
  37.8 20.7 %collective-permute-start.6 = (bf16[2,592,256]{2,1,0:T(8,128)(2,1)}, bf16[2,592,256]{2,1,0:T(8,128)(2,1)S(1)}, u32[]{:S(2)}, u32[]{:S(2)}) collective-permute-start(bf16[2,592,256]{2,1,0:T(8,128)(2,1)} %collective-permute-done.3.refs_0_), channel_id=1, source_target_pairs={{32,48},{48,32},{64,80},{80,64},{96,112},{112,96},{128,144},{144,1... | collective-permute-start | bytes 1818632 | tf_op jit(solution)/shard_map/ppermute | solution.py:187
  44.4 19.3 %collective-permute-start.7 = (bf16[2,592,256]{2,1,0:T(8,128)(2,1)S(1)}, bf16[2,592,256]{2,1,0:T(8,128)(2,1)S(1)}, u32[]{:S(2)}, u32[]{:S(2)}) collective-permute-start(bf16[2,592,256]{2,1,0:T(8,128)(2,1)S(1)} %collective-permute-done.4.refs_0_), channel_id=1, source_target_pairs={{8,232},{24,248},{64,96},{80,112},{96,128},{112,144},{128,160},{14... | collective-permute-start | bytes 1818632 | tf_op jit(solution)/shard_map/ppermute | solution.py:206
  63.7 7.0 %collective-permute-start.8 = (bf16[2,592,256]{2,1,0:T(8,128)(2,1)S(1)}, bf16[2,592,256]{2,1,0:T(8,128)(2,1)S(1)}, u32[]{:S(2)}, u32[]{:S(2)}) collective-permute-start(bf16[2,592,256]{2,1,0:T(8,128)(2,1)S(1)} %collective-permute-done.6.refs_0_), channel_id=1, source_target_pairs={{32,40},{48,56},{64,72},{80,88},{96,104},{112,120},{128,136},{144,... | collective-permute-start | bytes 1818632 | tf_op jit(solution)/shard_map/ppermute | solution.py:190
  73.7 7.0 %collective-permute-start.9 = (bf16[2,592,256]{2,1,0:T(8,128)(2,1)S(1)}, bf16[2,592,256]{2,1,0:T(8,128)(2,1)S(1)}, u32[]{:S(2)}, u32[]{:S(2)}) collective-permute-start(bf16[2,592,256]{2,1,0:T(8,128)(2,1)S(1)} %collective-permute-done.4.refs_0_), channel_id=1, source_target_pairs={{64,72},{80,88},{96,104},{112,120},{128,136},{144,152},{160,168},{... | collective-permute-start | bytes 1818632 | tf_op jit(solution)/shard_map/ppermute | solution.py:190
  78.1 18.4 %collective-permute-start.10 = (bf16[2,592,256]{2,1,0:T(8,128)(2,1)S(1)}, bf16[2,592,256]{2,1,0:T(8,128)(2,1)S(1)}, u32[]{:S(2)}, u32[]{:S(2)}) collective-permute-start(bf16[2,592,256]{2,1,0:T(8,128)(2,1)S(1)} %collective-permute-done.4.refs_0_), channel_id=1, source_target_pairs={{64,80},{80,64},{96,112},{112,96},{128,144},{144,128},{160,176},{1... | collective-permute-start | bytes 1818632 | tf_op jit(solution)/shard_map/ppermute | solution.py:187
  80.7 15.8 %collective-permute-start.11 = (bf16[2,592,256]{2,1,0:T(8,128)(2,1)S(1)}, bf16[2,592,256]{2,1,0:T(8,128)(2,1)S(1)}, u32[]{:S(2)}, u32[]{:S(2)}) collective-permute-start(bf16[2,592,256]{2,1,0:T(8,128)(2,1)S(1)} %collective-permute-done.7.refs_0_), channel_id=1, source_target_pairs={{96,104},{112,120},{128,136},{136,128},{144,152},{152,144},{160,16... | collective-permute-start | bytes 1818632 | tf_op jit(solution)/shard_map/ppermute | solution.py:190
  85.1 23.5 %collective-permute-start.12 = (bf16[2,592,256]{2,1,0:T(8,128)(2,1)S(1)}, bf16[2,592,256]{2,1,0:T(8,128)(2,1)S(1)}, u32[]{:S(2)}, u32[]{:S(2)}) collective-permute-start(bf16[2,592,256]{2,1,0:T(8,128)(2,1)S(1)} %collective-permute-done.7.refs_0_), channel_id=1, source_target_pairs={{96,112},{112,96},{128,144},{136,152},{144,128},{152,136},{160,176... | collective-permute-start | bytes 1818632 | tf_op jit(solution)/shard_map/ppermute | solution.py:187
  96.6 12.0 %collective-permute-start.13 = (bf16[2,592,256]{2,1,0:T(8,128)(2,1)S(1)}, bf16[2,592,256]{2,1,0:T(8,128)(2,1)S(1)}, u32[]{:S(2)}, u32[]{:S(2)}) collective-permute-start(bf16[2,592,256]{2,1,0:T(8,128)(2,1)S(1)} %collective-permute-done.10.refs_0_), channel_id=1, source_target_pairs={{64,72},{80,88},{96,104},{112,120},{128,136},{144,152},{160,168},{... | collective-permute-start | bytes 1818632 | tf_op jit(solution)/shard_map/ppermute | solution.py:190
  108.6 11.2 %copy-start.1 = (bf16[1,8,512,128]{3,2,1,0:T(8,128)(2,1)S(1)}, bf16[1,8,512,128]{3,2,1,0:T(8,128)(2,1)}, u32[]{:S(2)}) copy-start(bf16[1,8,512,128]{3,2,1,0:T(8,128)(2,1)} %param.9) | copy-start | bytes 3145732
  108.6 11.2 %collective-permute-start.14 = (bf16[2,592,256]{2,1,0:T(8,128)(2,1)S(1)}, bf16[2,592,256]{2,1,0:T(8,128)(2,1)S(1)}, u32[]{:S(2)}, u32[]{:S(2)}) collective-permute-start(bf16[2,592,256]{2,1,0:T(8,128)(2,1)S(1)} %collective-permute-done.12.refs_1_), channel_id=1, source_target_pairs={{96,104},{112,120},{128,136},{136,128},{144,152},{152,144},{160,16... | collective-permute-start | bytes 1818632 | tf_op jit(solution)/shard_map/ppermute | solution.py:190
  125.7 14.9 %collective-permute-start.15 = (bf16[1,256,1024]{2,1,0:T(8,128)(2,1)S(1)}, bf16[1,256,1024]{2,1,0:T(8,128)(2,1)S(1)}, u32[]{:S(2)}, u32[]{:S(2)}) collective-permute-start(bf16[1,256,1024]{2,1,0:T(8,128)(2,1)S(1)} %bitcast.22), channel_id=1, source_target_pairs={{0,1},{1,2},{2,3},{3,4},{4,5},{5,6},{6,7},{7,0},{8,9},{9,10},{10,1... | collective-permute-start | bytes 1572872 | tf_op jit(solution)/shard_map/ppermute | solution.py:253
